TPU v7x, 128 devices: a whole 4x4x4 slice. The times are simulated.
128 devices in a mesh: gx: 16 (over y, x), gy: 8 (over z, core).
Axes of the slice: x: 4, y: 4, z: 4, core: 2. Of those that a mesh axis runs over, the one named last changes fastest.
Arguments:
- composition: float32 [53, 1048576], P(None, ('gx', 'gy')), may hold values from -6 to 6
- particle_mass: float32 [1048576], P(('gx', 'gy')), may hold values from 0.3 to 3
- particle_cell: int32 [2, 1048576], P(None, ('gx', 'gy')), may hold values from 0 to 1023, as said below
- particle_level: int32 [1048576], P(('gx', 'gy')), may hold values from 0 to 2, as said below
- les_mean: float32 [53, 64, 1024], P(None, 'gx', 'gy'), may hold values from -6 to 6
- mix_rate: float32 [64, 1024], P('gx', 'gy'), may hold values from 0.1 to 3
- rate_matrix: float32 [3, 53, 53], replicated, may hold values from -0.875 to 0.875
- implicit_map: float32 [3, 53, 53], replicated, may hold values from -0.875 to 0.875
Outputs:
- updated: float32 [53, 1048576], P(None, ('gx', 'gy'))
- cell_means: float32 [53, 64, 1024], P(None, 'gx', 'gy')
Inputs may be any that keep to these rules, and one draw needn't show every extreme that they name: `particle_cell`: row 0 is below 64 and row 1 below 1024. With the cells split into blocks of 4 x 128 cells in device order (streamwise block index major), every particle's cell lies within 2 cells, in each grid direction, of the block of the device that holds the particle; the distance 2 is reached on every side that has a neighbouring block. `particle_level`: the share of full-mechanism particles differs from device to device, from none to all.
All inputs are finite; a program needn't handle non-finite values.
Results may differ from a plain program's by a relative error of at most 0.0001.
Values sent between devices are 32-bit elements; how exact they have to be, the bound alone decides.
No kernel may reach another device: no remote copies, remote signals or barrier semaphores. Data moves between devices by JAX's collectives and lax.ppermute only.
A program may use at most 64 MiB of HBM per device.

v0:
```python
import jax
import jax.numpy as jnp
from jax import lax
from jax.sharding import PartitionSpec as P

NS_LOW = 21
NS_MID = 24
R = 2


prior_weight = 16.0
chem_step = 0.5


def padded_2(cells, sides, width):
    for axis, dim in sides:
        count = lax.axis_size(axis)
        ends = count - 1
        head = lax.slice_in_dim(cells, 0, width, axis=dim)
        tail = lax.slice_in_dim(cells, cells.shape[dim] - width, cells.shape[dim], axis=dim)
        cells = jnp.concatenate(
            [
                lax.ppermute(tail, axis, [(i, (i + 1) % count) for i in range(ends)]),
                cells,
                lax.ppermute(head, axis, [((i + 1) % count, i) for i in range(ends)]),
            ],
            axis=dim,
        )
    return cells


def react_padded(mixed_comp, rate_matrix, implicit_map, particle_level):
    species_count = mixed_comp.shape[0]
    species_index = jnp.arange(species_count)
    updated = mixed_comp
    for tier_index, active in enumerate((NS_LOW, NS_MID, species_count)):
        keep_mask = (species_index < active).astype(jnp.float32)[:, None]
        source = keep_mask * jnp.tanh(
            jnp.dot(
                rate_matrix[tier_index],
                keep_mask * mixed_comp,
                precision=lax.Precision.HIGHEST,
                preferred_element_type=jnp.float32,
            )
        )
        change = keep_mask * jnp.dot(
            implicit_map[tier_index],
            source,
            precision=lax.Precision.HIGHEST,
            preferred_element_type=jnp.float32,
        )
        updated = updated + jnp.where(
            particle_level[None, :] == tier_index, chem_step * change, 0.0
        )
    return updated


def fold_in(field, dim, inner, from_above, from_below):
    interior = lax.slice_in_dim(field, R, R + inner, axis=dim)
    widths_above = [(0, 0)] * field.ndim
    widths_above[dim] = (inner - R, 0)
    widths_below = [(0, 0)] * field.ndim
    widths_below[dim] = (0, inner - R)
    return interior + jnp.pad(from_above, widths_above) + jnp.pad(from_below, widths_below)


def fold_margin(padded, dim, inner):
    span = inner + 2 * R
    middle = lax.slice_in_dim(padded, R, R + span, axis=dim)
    from_below = lax.slice_in_dim(padded, 0, R, axis=dim)
    from_above = lax.slice_in_dim(padded, span + R, span + 2 * R, axis=dim)
    return fold_in(middle, dim, inner, from_above, from_below)


def per_device(
    composition,
    particle_mass,
    particle_cell,
    particle_level,
    les_mean,
    mix_rate,
    rate_matrix,
    implicit_map,
):
    species_count = composition.shape[0]
    block_x = les_mean.shape[1]
    block_y = les_mean.shape[2]
    column_index = lax.axis_index("gx")
    row_index = lax.axis_index("gy")
    cell_x = particle_cell[0]
    cell_y = particle_cell[1]
    span_x = block_x + 2 * R
    span_y = block_y + 2 * R
    local_x = cell_x - (column_index * block_x - R)
    local_y = cell_y - (row_index * block_y - R)
    ext_index = local_x * span_y + local_y
    weighted = composition * particle_mass[None, :]
    ext_sums = (
        jnp.zeros((species_count, span_x * span_y), jnp.float32).at[:, ext_index].add(weighted)
    )
    ext_mass = (
        jnp.zeros((1, span_x * span_y), jnp.float32).at[:, ext_index].add(particle_mass[None, :])
    )
    ext_sums = ext_sums.reshape(species_count, span_x, span_y)
    ext_mass = ext_mass.reshape(1, span_x, span_y)
    wide_sums, wide_mass = (
        padded_2(ext_sums, (("gx", 1), ("gy", 2)), R),
        padded_2(ext_mass, (("gx", 1), ("gy", 2)), R),
    )
    part_sums = fold_margin(fold_margin(wide_sums, 1, block_x), 2, block_y)
    part_mass = fold_margin(fold_margin(wide_mass, 1, block_x), 2, block_y)
    cell_means = (part_sums + prior_weight * les_mean) / (part_mass + prior_weight)
    ext_means, ext_rate = (
        padded_2(cell_means, (("gx", 1), ("gy", 2)), R),
        padded_2(mix_rate[None], (("gx", 1), ("gy", 2)), R),
    )
    particle_means = jnp.take(ext_means.reshape(species_count, span_x * span_y), ext_index, axis=1)
    particle_rate = jnp.take(ext_rate.reshape(span_x * span_y), ext_index, axis=0)
    factor = 1.0 - jnp.exp(-particle_rate)
    mixed_comp = composition - factor[None, :] * (composition - particle_means)
    updated = react_padded(mixed_comp, rate_matrix, implicit_map, particle_level)
    return (updated, cell_means)


def solution(mesh):
    placed = (
        P(None, ("gx", "gy")),
        P(("gx", "gy")),
        P(None, ("gx", "gy")),
        P(("gx", "gy")),
        P(None, "gx", "gy"),
        P("gx", "gy"),
        P(),
        P(),
    )
    return jax.shard_map(
        per_device,
        mesh=mesh,
        in_specs=placed,
        out_specs=(P(None, ("gx", "gy")), P(None, "gx", "gy")),
        check_vma=False,
    )
```

profile of v0, /device:TPU:24, one launch (start us, length us, event | category | flops | bytes accessed | tf_op | source)
XLA Modules:
  0.0 262.1 jit_solution(11327790382592899734)
XLA Ops:
  1.6 56.8 %scatter_custom_fusion.1 = f32[1056]{0:T(1024)S(1)} fusion(s32[8192]{0:T(1024)S(1)} %bitcast.52, f32[8192]{0:T(1024)} %param.9, f32[]{:T(128)} %constant.40.clone.1), kind=kCustom, calls=%fused_computation.101 | custom fusion | flops 8192 | bytes 4736 | tf_op jit(solution)/shard_map/scatter-add | solution.py:102
  58.5 3.4 %collective-permute-start.8 = (f32[1,2,132]{2,1,0:T(2,128)S(1)}, f32[1,2,132]{2,1,0:T(2,128)S(1)}, u32[]{:S(2)}, u32[]{:S(2)}) collective-permute-start(f32[1,2,132]{2,1,0:T(2,128)S(1)} %get-tuple-element.17), channel_id=1, source_target_pairs={{0,8},{8,16},{16,24},{24,32},{32,40},{40,48},{48,56},{56,64},{64,7... | collective-permute-start | bytes 3176 | tf_op jit(solution)/shard_map/ppermute | solution.py:23
  62.0 4.5 %collective-permute-start.9 = (f32[1,2,132]{2,1,0:T(2,128)S(1)}, f32[1,2,132]{2,1,0:T(2,128)S(1)}, u32[]{:S(2)}, u32[]{:S(2)}) collective-permute-start(f32[1,2,132]{2,1,0:T(2,128)S(1)} %get-tuple-element.18), channel_id=1, source_target_pairs={{8,0},{16,8},{24,16},{32,24},{40,32},{48,40},{56,48},{64,56},{72,6... | collective-permute-start | bytes 3176 | tf_op jit(solution)/shard_map/ppermute | solution.py:25
  66.5 1.6 multiply_bitcast_fusion
  68.2 2.8 %copy.16 = f32[8192,53]{1,0:T(8,128)} copy(f32[8192,53]{0,1:T(8,128)S(1)} %multiply_bitcast_fusion) | data formatting | bytes 3473408 | tf_op jit(solution)/shard_map/mul | solution.py:97
  70.9 44.4 %scatter_custom_fusion = f32[53,1056]{0,1:T(8,128)S(1)} fusion(s32[8192]{0:T(1024)S(1)} %bitcast.53, f32[8192,53]{1,0:T(8,128)} %copy.16, f32[]{:T(128)} %constant.40.clone.1), kind=kCustom, calls=%fused_computation.37 | custom fusion | flops 434176 | bytes 224384 | tf_op jit(solution)/shard_map/scatter-add | solution.py:99
  116.0 1.9 collective-permute-start.4
  117.9 2.7 %collective-permute-start = (f32[1,2,128]{2,1,0:T(2,128)S(1)}, f32[1,2,128]{2,1,0:T(2,128)S(1)}, u32[]{:S(2)}, u32[]{:S(2)}) collective-permute-start(f32[1,2,128]{2,1,0:T(2,128)S(1)} %get-tuple-element.21), channel_id=1, source_target_pairs={{0,8},{8,16},{16,24},{24,32},{32,40},{40,48},{48,56},{56,64},{64,7... | collective-permute-start | bytes 3080 | tf_op jit(solution)/shard_map/ppermute | solution.py:23
  120.7 5.2 %collective-permute-start.1 = (f32[1,2,128]{2,1,0:T(2,128)S(1)}, f32[1,2,128]{2,1,0:T(2,128)S(1)}, u32[]{:S(2)}, u32[]{:S(2)}) collective-permute-start(f32[1,2,128]{2,1,0:T(2,128)S(1)} %get-tuple-element.22), channel_id=1, source_target_pairs={{8,0},{16,8},{24,16},{32,24},{40,32},{48,40},{56,48},{64,56},{72,6... | collective-permute-start | bytes 3080 | tf_op jit(solution)/shard_map/ppermute | solution.py:25
  126.0 3.9 %collective-permute-start.5 = (f32[53,2,132]{2,1,0:T(2,128)S(1)}, f32[53,2,132]{2,1,0:T(2,128)S(1)}, u32[]{:S(2)}, u32[]{:S(2)}) collective-permute-start(f32[53,2,132]{2,1,0:T(2,128)S(1)} %get-tuple-element.7), channel_id=1, source_target_pairs={{8,0},{16,8},{24,16},{32,24},{40,32},{48,40},{56,48},{64,56},{72,6... | collective-permute-start | bytes 167912 | tf_op jit(solution)/shard_map/ppermute | solution.py:25
  130.1 1.3 collective-permute-start.2
  131.5 4.5 %collective-permute-start.10 = (f32[1,12,2]{2,1,0:T(8,128)S(1)}, f32[1,12,2]{2,1,0:T(8,128)S(1)}, u32[]{:S(2)}, u32[]{:S(2)}) collective-permute-start(f32[1,12,2]{2,1,0:T(8,128)S(1)} %get-tuple-element.15), channel_id=1, source_target_pairs={{0,1},{1,2},{2,3},{3,4},{4,5},{5,6},{6,7},{8,9},{9,10},{10,11},{11... | collective-permute-start | bytes 296 | tf_op jit(solution)/shard_map/ppermute | solution.py:23
  136.0 1.3 collective-permute-start.11
  137.3 1.3 collective-permute-start.3
  139.6 4.1 %collective-permute-start.6 = (f32[53,12,2]{2,1,0:T(8,128)S(1)}, f32[53,12,2]{2,1,0:T(8,128)S(1)}, u32[]{:S(2)}, u32[]{:S(2)}) collective-permute-start(f32[53,12,2]{2,1,0:T(8,128)S(1)} %get-tuple-element.4), channel_id=1, source_target_pairs={{0,1},{1,2},{2,3},{3,4},{4,5},{5,6},{6,7},{8,9},{9,10},{10,11},{11... | collective-permute-start | bytes 15272 | tf_op jit(solution)/shard_map/ppermute | solution.py:23
  143.8 1.3 collective-permute-start.7
  145.2 2.6 collective-permute-done.7
  149.2 1.9 collective-permute-start.12
  151.1 6.0 %collective-permute-start.13 = (f32[53,2,128]{2,1,0:T(2,128)S(1)}, f32[53,2,128]{2,1,0:T(2,128)S(1)}, u32[]{:S(2)}, u32[]{:S(2)}) collective-permute-start(f32[53,2,128]{2,1,0:T(2,128)S(1)} %get-tuple-element.11), channel_id=1, source_target_pairs={{8,0},{16,8},{24,16},{32,24},{40,32},{48,40},{56,48},{64,56},{72,6... | collective-permute-start | bytes 162824 | tf_op jit(solution)/shard_map/ppermute | solution.py:25
  157.4 45.5 %gather_fusion = f32[8192]{0:T(1024)S(1)} fusion(f32[1056]{0:T(1024)S(1)} %reshape.96, s32[8192]{0:T(1024)S(1)} %broadcast_clamp_fusion), kind=kCustom, calls=%fused_computation | custom fusion | bytes 98304 | tf_op jit(solution)/shard_map/jit(_take)/gather | solution.py:118
  203.1 7.7 %collective-permute-start.14 = (f32[53,8,2]{2,1,0:T(8,128)S(1)}, f32[53,8,2]{2,1,0:T(8,128)S(1)}, u32[]{:S(2)}, u32[]{:S(2)}) collective-permute-start(f32[53,8,2]{2,1,0:T(8,128)S(1)} %get-tuple-element.8), channel_id=1, source_target_pairs={{0,1},{1,2},{2,3},{3,4},{4,5},{5,6},{6,7},{8,9},{9,10},{10,11},{11... | collective-permute-start | bytes 10184 | tf_op jit(solution)/shard_map/ppermute | solution.py:23
  210.9 1.3 collective-permute-start.15
  212.3 1.9 collective-permute-done.15
  215.1 27.7 %gather_fusion.1 = f32[8192,53]{1,0:T(8,128)} fusion(f32[53,1056]{0,1:T(8,128)S(1)} %copy.18, s32[8192]{0:T(1024)S(1)} %broadcast_clamp_fusion), kind=kCustom, calls=%fused_computation.1 | custom fusion | bytes 3506176 | tf_op jit(solution)/shard_map/jit(_take)/gather | solution.py:117
  242.9 3.9 %copy.19 = f32[8192,53]{0,1:T(8,128)} copy(f32[8192,53]{1,0:T(8,128)} %gather_fusion.1) | data formatting | bytes 3473408 | tf_op jit(solution)/shard_map/jit(_take)/gather | solution.py:117
  246.8 1.8 fusion.16
  248.6 2.0 fusion.14
  250.7 2.0 fusion.9
  252.7 2.0 fusion.4
  254.8 2.0 fusion.13
  256.8 2.0 fusion.8
  258.9 3.3 %fusion.3 = f32[53,8192]{1,0:T(8,128)} fusion(f32[53,8192]{1,0:T(8,128)S(1)} %fusion.8, f32[8192,53]{0,1:T(8,128)S(1)} %fusion.4, f32[53]{0:T(128)S(1)} %compare_convert_fusion, pred[8192]{0:T(1024)(128)(4,1)S(1)} %get-tuple-element.12, f32[3,53,53]{2,1,0:T(8,128)S(1)} %copy-done.4), kind=kOutput, calls=%fused_computation.8 | convolution fusion | flops 277872640 | bytes 5444096 | tf_op jit(solution)/shard_map/dot_general | solution.py:46
  (66 shorter events, 5.8 us)
Async XLA Ops:
  58.5 72.8 %collective-permute-start.8 = (f32[1,2,132]{2,1,0:T(2,128)S(1)}, f32[1,2,132]{2,1,0:T(2,128)S(1)}, u32[]{:S(2)}, u32[]{:S(2)}) collective-permute-start(f32[1,2,132]{2,1,0:T(2,128)S(1)} %get-tuple-element.17), channel_id=1, source_target_pairs={{0,8},{8,16},{16,24},{24,32},{32,40},{40,48},{48,56},{56,64},{64,7... | collective-permute-start | bytes 3176 | tf_op jit(solution)/shard_map/ppermute | solution.py:23
  62.0 69.4 %collective-permute-start.9 = (f32[1,2,132]{2,1,0:T(2,128)S(1)}, f32[1,2,132]{2,1,0:T(2,128)S(1)}, u32[]{:S(2)}, u32[]{:S(2)}) collective-permute-start(f32[1,2,132]{2,1,0:T(2,128)S(1)} %get-tuple-element.18), channel_id=1, source_target_pairs={{8,0},{16,8},{24,16},{32,24},{40,32},{48,40},{56,48},{64,56},{72,6... | collective-permute-start | bytes 3176 | tf_op jit(solution)/shard_map/ppermute | solution.py:25
  70.9 47.0 %copy-start.6 = (f32[4,128]{1,0:T(4,128)S(1)}, f32[4,128]{1,0:T(4,128)}, u32[]{:S(2)}) copy-start(f32[4,128]{1,0:T(4,128)} %param.13) | copy-start | bytes 6148
  70.9 55.1 %copy-start.5 = (s32[8192]{0:T(1024)S(1)}, s32[8192]{0:T(1024)}, u32[]{:S(2)}) copy-start(s32[8192]{0:T(1024)} %param.11) | copy-start | bytes 98308
  70.9 68.2 %copy-start.7 = (pred[4]{0:T(512)(128)(4,1)S(1)}, pred[4]{0:T(512)(128)(4,1)}, u32[]{:S(2)}) copy-start(pred[4]{0:T(512)(128)(4,1)} %constant.70.clone.1) | copy-start | bytes 16
  116.0 29.1 %copy-start.8 = (pred[128]{0:T(512)(128)(4,1)S(1)}, pred[128]{0:T(512)(128)(4,1)}, u32[]{:S(2)}) copy-start(pred[128]{0:T(512)(128)(4,1)} %constant.71.clone.1) | copy-start | bytes 388
  116.0 23.3 %collective-permute-start.4 = (f32[53,2,132]{2,1,0:T(2,128)S(1)}, f32[53,2,132]{2,1,0:T(2,128)S(1)}, u32[]{:S(2)}, u32[]{:S(2)}) collective-permute-start(f32[53,2,132]{2,1,0:T(2,128)S(1)} %get-tuple-element.6), channel_id=1, source_target_pairs={{0,8},{8,16},{16,24},{24,32},{32,40},{40,48},{48,56},{56,64},{64,7... | collective-permute-start | bytes 167912 | tf_op jit(solution)/shard_map/ppermute | solution.py:23
  117.9 8.1 %collective-permute-start = (f32[1,2,128]{2,1,0:T(2,128)S(1)}, f32[1,2,128]{2,1,0:T(2,128)S(1)}, u32[]{:S(2)}, u32[]{:S(2)}) collective-permute-start(f32[1,2,128]{2,1,0:T(2,128)S(1)} %get-tuple-element.21), channel_id=1, source_target_pairs={{0,8},{8,16},{16,24},{24,32},{32,40},{40,48},{48,56},{56,64},{64,7... | collective-permute-start | bytes 3080 | tf_op jit(solution)/shard_map/ppermute | solution.py:23
  120.7 9.3 %collective-permute-start.1 = (f32[1,2,128]{2,1,0:T(2,128)S(1)}, f32[1,2,128]{2,1,0:T(2,128)S(1)}, u32[]{:S(2)}, u32[]{:S(2)}) collective-permute-start(f32[1,2,128]{2,1,0:T(2,128)S(1)} %get-tuple-element.22), channel_id=1, source_target_pairs={{8,0},{16,8},{24,16},{32,24},{40,32},{48,40},{56,48},{64,56},{72,6... | collective-permute-start | bytes 3080 | tf_op jit(solution)/shard_map/ppermute | solution.py:25
  126.0 13.2 %collective-permute-start.5 = (f32[53,2,132]{2,1,0:T(2,128)S(1)}, f32[53,2,132]{2,1,0:T(2,128)S(1)}, u32[]{:S(2)}, u32[]{:S(2)}) collective-permute-start(f32[53,2,132]{2,1,0:T(2,128)S(1)} %get-tuple-element.7), channel_id=1, source_target_pairs={{8,0},{16,8},{24,16},{32,24},{40,32},{48,40},{56,48},{64,56},{72,6... | collective-permute-start | bytes 167912 | tf_op jit(solution)/shard_map/ppermute | solution.py:25
  130.1 27.1 %collective-permute-start.2 = (f32[1,8,2]{2,1,0:T(8,128)S(1)}, f32[1,8,2]{2,1,0:T(8,128)S(1)}, u32[]{:S(2)}, u32[]{:S(2)}) collective-permute-start(f32[1,8,2]{2,1,0:T(8,128)S(1)} %get-tuple-element.19), channel_id=1, source_target_pairs={{0,1},{1,2},{2,3},{3,4},{4,5},{5,6},{6,7},{8,9},{9,10},{10,11},{11... | collective-permute-start | bytes 200 | tf_op jit(solution)/shard_map/ppermute | solution.py:23
  131.5 5.9 %collective-permute-start.10 = (f32[1,12,2]{2,1,0:T(8,128)S(1)}, f32[1,12,2]{2,1,0:T(8,128)S(1)}, u32[]{:S(2)}, u32[]{:S(2)}) collective-permute-start(f32[1,12,2]{2,1,0:T(8,128)S(1)} %get-tuple-element.15), channel_id=1, source_target_pairs={{0,1},{1,2},{2,3},{3,4},{4,5},{5,6},{6,7},{8,9},{9,10},{10,11},{11... | collective-permute-start | bytes 296 | tf_op jit(solution)/shard_map/ppermute | solution.py:23
  136.0 3.1 %collective-permute-start.11 = (f32[1,12,2]{2,1,0:T(8,128)S(1)}, f32[1,12,2]{2,1,0:T(8,128)S(1)}, u32[]{:S(2)}, u32[]{:S(2)}) collective-permute-start(f32[1,12,2]{2,1,0:T(8,128)S(1)} %get-tuple-element.16), channel_id=1, source_target_pairs={{1,0},{2,1},{3,2},{4,3},{5,4},{6,5},{7,6},{9,8},{10,9},{11,10},{12... | collective-permute-start | bytes 296 | tf_op jit(solution)/shard_map/ppermute | solution.py:25
  137.3 19.9 %collective-permute-start.3 = (f32[1,8,2]{2,1,0:T(8,128)S(1)}, f32[1,8,2]{2,1,0:T(8,128)S(1)}, u32[]{:S(2)}, u32[]{:S(2)}) collective-permute-start(f32[1,8,2]{2,1,0:T(8,128)S(1)} %get-tuple-element.20), channel_id=1, source_target_pairs={{1,0},{2,1},{3,2},{4,3},{5,4},{6,5},{7,6},{9,8},{10,9},{11,10},{12... | collective-permute-start | bytes 200 | tf_op jit(solution)/shard_map/ppermute | solution.py:25
  139.4 9.5 %copy-start.2 = (f32[53,4,128]{2,1,0:T(4,128)S(1)}, f32[53,4,128]{2,1,0:T(4,128)}, u32[]{:S(2)}) copy-start(f32[53,4,128]{2,1,0:T(4,128)} %param.12) | copy-start | bytes 325636
  139.6 5.5 %collective-permute-start.6 = (f32[53,12,2]{2,1,0:T(8,128)S(1)}, f32[53,12,2]{2,1,0:T(8,128)S(1)}, u32[]{:S(2)}, u32[]{:S(2)}) collective-permute-start(f32[53,12,2]{2,1,0:T(8,128)S(1)} %get-tuple-element.4), channel_id=1, source_target_pairs={{0,1},{1,2},{2,3},{3,4},{4,5},{5,6},{6,7},{8,9},{9,10},{10,11},{11... | collective-permute-start | bytes 15272 | tf_op jit(solution)/shard_map/ppermute | solution.py:23
  143.8 4.0 %collective-permute-start.7 = (f32[53,12,2]{2,1,0:T(8,128)S(1)}, f32[53,12,2]{2,1,0:T(8,128)S(1)}, u32[]{:S(2)}, u32[]{:S(2)}) collective-permute-start(f32[53,12,2]{2,1,0:T(8,128)S(1)} %get-tuple-element.5), channel_id=1, source_target_pairs={{1,0},{2,1},{3,2},{4,3},{5,4},{6,5},{7,6},{9,8},{10,9},{11,10},{12... | collective-permute-start | bytes 15272 | tf_op jit(solution)/shard_map/ppermute | solution.py:25
  149.1 65.1 %copy-start.1 = (f32[53,4,128]{2,1,0:T(4,128)}, f32[53,4,128]{2,1,0:T(4,128)S(1)}, u32[]{:S(2)}) copy-start(f32[53,4,128]{2,1,0:T(4,128)S(1)} %fusion.35) | copy-start | bytes 325636
  149.2 53.7 %collective-permute-start.12 = (f32[53,2,128]{2,1,0:T(2,128)S(1)}, f32[53,2,128]{2,1,0:T(2,128)S(1)}, u32[]{:S(2)}, u32[]{:S(2)}) collective-permute-start(f32[53,2,128]{2,1,0:T(2,128)S(1)} %get-tuple-element.10), channel_id=1, source_target_pairs={{0,8},{8,16},{16,24},{24,32},{32,40},{40,48},{48,56},{56,64},{64,7... | collective-permute-start | bytes 162824 | tf_op jit(solution)/shard_map/ppermute | solution.py:23
  151.1 51.8 %collective-permute-start.13 = (f32[53,2,128]{2,1,0:T(2,128)S(1)}, f32[53,2,128]{2,1,0:T(2,128)S(1)}, u32[]{:S(2)}, u32[]{:S(2)}) collective-permute-start(f32[53,2,128]{2,1,0:T(2,128)S(1)} %get-tuple-element.11), channel_id=1, source_target_pairs={{8,0},{16,8},{24,16},{32,24},{40,32},{48,40},{56,48},{64,56},{72,6... | collective-permute-start | bytes 162824 | tf_op jit(solution)/shard_map/ppermute | solution.py:25
  203.1 9.1 %collective-permute-start.14 = (f32[53,8,2]{2,1,0:T(8,128)S(1)}, f32[53,8,2]{2,1,0:T(8,128)S(1)}, u32[]{:S(2)}, u32[]{:S(2)}) collective-permute-start(f32[53,8,2]{2,1,0:T(8,128)S(1)} %get-tuple-element.8), channel_id=1, source_target_pairs={{0,1},{1,2},{2,3},{3,4},{4,5},{5,6},{6,7},{8,9},{9,10},{10,11},{11... | collective-permute-start | bytes 10184 | tf_op jit(solution)/shard_map/ppermute | solution.py:23
  210.9 3.4 %collective-permute-start.15 = (f32[53,8,2]{2,1,0:T(8,128)S(1)}, f32[53,8,2]{2,1,0:T(8,128)S(1)}, u32[]{:S(2)}, u32[]{:S(2)}) collective-permute-start(f32[53,8,2]{2,1,0:T(8,128)S(1)} %get-tuple-element.9), channel_id=1, source_target_pairs={{1,0},{2,1},{3,2},{4,3},{5,4},{6,5},{7,6},{9,8},{10,9},{11,10},{12... | collective-permute-start | bytes 10184 | tf_op jit(solution)/shard_map/ppermute | solution.py:25
  242.9 3.9 %copy-start = (f32[53,8192]{1,0:T(8,128)S(1)}, f32[53,8192]{1,0:T(8,128)}, u32[]{:S(2)}) copy-start(f32[53,8192]{1,0:T(8,128)} %param.8) | copy-start | bytes 5210116
  246.8 1.8 copy-start.3
  252.7 2.0 copy-start.4
where the time goes:
time: 267 us; the launch traced here: 262 us
  other arithmetic  108 us (40%)
  local copies, waits for them, and re-layouts  81.9 us (31%)
  starting transfers between devices  52.5 us (20%)
  matrix products  13.4 us (5%)
  waiting for transfers between devices  5.04 us (2%)
    scatter-add x1, other arithmetic, per_device(): jnp.zeros((1, span_x * span_y), jnp.float32).at[:, ext_index]  56.8 us
    gather x1, local copies, waits for them, and re-layouts, per_device(): jnp.take(ext_rate.reshape(span_x * span_y), ext_index, axis=0)  45.5 us
    scatter-add x1, other arithmetic, per_device(): jnp.zeros((species_count, span_x * span_y), jnp.float32).at[:, ext_index]  44.4 us
    gather x2, local copies, waits for them, and re-layouts, per_device(): jnp.take(ext_means.reshape(species_count, span_x * span_y), ext_index, ax...  31.7 us
    ppermute x8, starting transfers between devices, padded_2(): lax.ppermute(tail, axis, [(i, (i + 1) % count) for i in range(ends)])  27.7 us
    ppermute x8, starting transfers between devices, padded_2(): lax.ppermute(head, axis, [((i + 1) % count, i) for i in range(ends)])  24.9 us
    dot_general x3, matrix products, react_padded(): jnp.dot(implicit_map[tier_index], source, precision=lax.Precision.HIGHEST...  7.35 us
    dot_general x3, matrix products, react_padded(): jnp.dot(rate_matrix[tier_index], keep_mask * mixed_comp, precision=lax.Pr...  6.08 us
  transfers between devices with their start and end apart: 16, of which 3 were waited for; matrix products, arithmetic and copies ran while one was open for 37% of the time, Pallas kernels for 0%

commit v1 on v0

v1 whole, which is shorter than its diff:
```python
import functools

import jax
import jax.numpy as jnp
from jax import lax
from jax.experimental import pallas as pl
from jax.experimental.pallas import tpu as pltpu
from jax.sharding import PartitionSpec as P

NS_LOW = 21
NS_MID = 24
NSP = 53
R = 2
CX = 4
CY = 128
ROWS = 56
GROUPS = 4
CHUNK = 1024

prior_weight = 16.0
chem_step = 0.5

f32 = jnp.float32
bf16 = jnp.bfloat16


def split(x):
    high = x.astype(bf16).astype(f32)
    return high, x - high


def stacked(x):
    high, low = split(x)
    return jnp.concatenate([high, low], axis=0).astype(bf16)


def local_cells(cell_ref):
    local_x = cell_ref[0:1, :] - (lax.axis_index("gx") * CX - R)
    local_y = cell_ref[1:2, :] - (lax.axis_index("gy") * CY - R)
    return local_x, local_y


def main_index(local_x, local_y):
    inside = (local_y >= 2 * R) & (local_y < CY)
    return jnp.where(inside, (local_x & 1) * CY + local_y - R, -1)


def edge_index(local_x, local_y):
    low = local_y < 2 * R
    high = local_y >= CY
    place = jnp.where(low, local_y, local_y - CY + 16)
    return jnp.where(low | high, (local_x >> 2) * 32 + (local_x & 3) * 4 + place, -1)


def hot(index, count):
    cells = lax.broadcasted_iota(jnp.int32, (count, index.shape[1]), 0)
    return jnp.where(cells == index, 1.0, 0.0).astype(bf16)


def dot_nt(a, b):
    return lax.dot_general(a, b, (((1,), (1,)), ((), ())), preferred_element_type=f32)


def dot(a, b):
    return jnp.dot(a, b, preferred_element_type=f32)


def sums_kernel(comp_ref, mass_ref, cell_ref, les_ref, rate_ref, main_ref, edge_ref, w_ref):
    step = pl.program_id(0)

    @pl.when(step == 0)
    def _():
        main_ref[...] = jnp.zeros_like(main_ref)
        edge_ref[...] = jnp.zeros_like(edge_ref)
        w_ref[...] = jnp.zeros_like(w_ref)
        lane = lax.broadcasted_iota(jnp.int32, (ROWS, CY), 1)
        inner = (lane >= R) & (lane < CY - R)
        column = lax.broadcasted_iota(jnp.int32, (1, CY), 1)
        for x in range(CX):
            w_ref[0:NSP, 0:CY] = prior_weight * les_ref[:, x, :]
            w_ref[NSP : NSP + 1, 0:CY] = jnp.full((1, CY), prior_weight, f32)
            w_ref[NSP + 1 : NSP + 2, 0:CY] = rate_ref[x : x + 1, :]
            own = w_ref[:, 0:CY]
            group, odd = divmod(x + R, 2)
            main_ref[group * ROWS : (group + 1) * ROWS, odd * CY : (odd + 1) * CY] = jnp.where(
                inner, own, 0.0
            )
            place = hot(edge_index(jnp.full((1, CY), x + R, jnp.int32), column + R), 128)
            both = dot_nt(stacked(own), place)
            edge_ref[...] += both[0:ROWS] + both[ROWS:]
        w_ref[...] = jnp.zeros_like(w_ref)

    mass = mass_ref[...].reshape(1, CHUNK)
    w_ref[0:NSP, :] = comp_ref[...] * mass
    w_ref[NSP : NSP + 1, :] = mass
    w = stacked(w_ref[...])
    local_x, local_y = local_cells(cell_ref)
    place = hot(main_index(local_x, local_y), 2 * CY)
    for group in range(GROUPS):
        mask = jnp.where((local_x >> 1) == group, 1.0, 0.0).astype(bf16)
        both = dot_nt(w * mask, place)
        main_ref[group * ROWS : (group + 1) * ROWS, :] += both[0:ROWS] + both[ROWS:]
    both = dot_nt(w, hot(edge_index(local_x, local_y), 128))
    edge_ref[...] += both[0:ROWS] + both[ROWS:]


def pack_kernel(main_ref, edge_ref, even_in_ref, odd_in_ref, even_ref, odd_ref):
    odd_y = lax.axis_index("gy") % 2 == 1
    odd_x = lax.axis_index("gx") % 2 == 1
    even_in = even_in_ref[...]
    odd_in = odd_in_ref[...]
    upper = jnp.where(odd_y, odd_in, even_in)
    lower = jnp.where(odd_y, even_in, odd_in)
    lane = lax.broadcasted_iota(jnp.int32, (ROWS, 128), 1)
    high = (lane & 16) != 0
    edge = edge_ref[...] + jnp.where(high, pltpu.roll(upper, 16, 1), pltpu.roll(lower, 112, 1))
    half = 2 * ROWS
    left, right = main_ref[0:half, :], main_ref[half:, :]
    even_ref[0:half, :] = jnp.where(odd_x, left, right)
    odd_ref[0:half, :] = jnp.where(odd_x, right, left)
    left_edge, right_edge = edge, pltpu.roll(edge, 96, 1)
    quarter = lane[0:8] >> 5
    for ref, part in (
        (even_ref, jnp.where(odd_x, left_edge, right_edge)),
        (odd_ref, jnp.where(odd_x, right_edge, left_edge)),
    ):
        for side in range(2):
            packed = jnp.zeros((8, 128), f32)
            for k in range(4):
                block = side * 4 + k
                if block < ROWS // 8:
                    rows = part[block * 8 : block * 8 + 8]
                    moved = pltpu.roll(rows, 32 * k, 1) if k else rows
                    packed = jnp.where(quarter == k, moved, packed)
            ref[half : half + 8, side * 128 : (side + 1) * 128] = packed


def table(total):
    rows = lax.broadcasted_iota(jnp.int32, total.shape, 0)
    mass = total[NSP : NSP + 1]
    mass = jnp.where(mass > 0.0, mass, 1.0)
    means = total / mass
    keep = jnp.exp(-total[NSP + 1 : NSP + 2])
    return means, jnp.where(rows < NSP, (1.0 - keep) * means, jnp.where(rows == NSP, keep, 0.0))


def unpacked(packed):
    lane = lax.broadcasted_iota(jnp.int32, (8, 128), 1)
    blocks = []
    for block in range(ROWS // 8):
        side, k = divmod(block, 4)
        rows = packed[:, side * 128 : (side + 1) * 128]
        rows = pltpu.roll(rows, 128 - 32 * k, 1) if k else rows
        blocks.append(jnp.where(lane < 32, rows, 0.0))
    return jnp.concatenate(blocks, axis=0)


def operator_rows(matrix_ref, full_ref, out_ref, scale):
    full_ref[...] = jnp.zeros_like(full_ref)
    start = 0
    for level, active in enumerate((NS_LOW, NS_MID, NSP)):
        rows = -(-active // 8) * 8
        count = min(rows, NSP)
        row = lax.broadcasted_iota(jnp.int32, (count, NSP), 0)
        col = lax.broadcasted_iota(jnp.int32, (count, NSP), 1)
        block = matrix_ref[level, 0:count, :] * scale
        high, low = split(jnp.where((row < active) & (col < active), block, 0.0))
        full_ref[start : start + count, 0:NSP] = high
        full_ref[start : start + count, 64 : 64 + NSP] = high
        full_ref[start : start + count, 128 : 128 + NSP] = low
        start += rows
    out_ref[...] = full_ref[...].astype(bf16)


def three(x):
    high, low = split(x)
    return jnp.concatenate([high, low, high], axis=0).astype(bf16)


def react_kernel(
    even_ref,
    odd_ref,
    even_in_ref,
    odd_in_ref,
    rate_ref,
    map_ref,
    comp_ref,
    cell_ref,
    level_ref,
    updated_ref,
    means_ref,
    high_ref,
    low_ref,
    edge_ref,
    full_ref,
    ops_ref,
    maps_ref,
    mixed_ref,
):
    step = pl.program_id(0)
    half = 2 * ROWS

    @pl.when(step == 0)
    def _():
        odd_x = lax.axis_index("gx") % 2 == 1
        even = even_ref[...] + even_in_ref[...]
        odd = odd_ref[...] + odd_in_ref[...]
        left = jnp.where(odd_x, even, odd)
        right = jnp.where(odd_x, odd, even)
        edge = unpacked(left[half:, :]) + pltpu.roll(unpacked(right[half:, :]), 32, 1)
        edge_means, edge_table = table(edge)
        high, low = split(edge_table)
        lane = lax.broadcasted_iota(jnp.int32, (ROWS, 128), 1)
        edge_ref[...] = jnp.where(lane < 64, high, pltpu.roll(low, 64, 1)).astype(bf16)
        high, low = split(edge_means)
        edge_means = jnp.where(lane < 64, high, pltpu.roll(low, 64, 1)).astype(bf16)
        row = lax.broadcasted_iota(jnp.int32, (128, CY), 0) & 63
        col = lax.broadcasted_iota(jnp.int32, (1, CY), 1)
        inner = (lane >= R) & (lane < CY - R)
        for group in range(GROUPS):
            source = left if group < 2 else right
            start = (group % 2) * ROWS
            means, cells = table(source[start : start + ROWS])
            high, low = split(cells)
            high_ref[group * ROWS : (group + 1) * ROWS, :] = high
            low_ref[group * ROWS : (group + 1) * ROWS, :] = low
            if group in (1, 2):
                for odd_column in range(2):
                    x = group * 2 + odd_column - R
                    index = edge_index(jnp.full((1, CY), x + R, jnp.int32), col + R)
                    placed = dot(edge_means, jnp.where(row == index, 1.0, 0.0).astype(bf16))
                    own = jnp.where(inner, means[:, odd_column * CY : (odd_column + 1) * CY], placed)
                    means_ref[:, x, :] = own[0:NSP]
        operator_rows(rate_ref, full_ref, ops_ref, 1.0)
        operator_rows(map_ref, full_ref, maps_ref, chem_step)
        mixed_ref[...] = jnp.zeros_like(mixed_ref)

    local_x, local_y = local_cells(cell_ref)
    place = hot(main_index(local_x, local_y), 2 * CY)
    gathered = dot(high_ref[...].astype(bf16), place) + dot(low_ref[...].astype(bf16), place)
    edge_cells = edge_index(local_x, local_y)
    row = lax.broadcasted_iota(jnp.int32, (128, CHUNK), 0) & 63
    value = dot(edge_ref[...], jnp.where(row == edge_cells, 1.0, 0.0).astype(bf16))
    group_of = local_x >> 1
    chosen = gathered[0:ROWS]
    for group in range(1, GROUPS):
        chosen = jnp.where(group_of == group, gathered[group * ROWS : (group + 1) * ROWS], chosen)
    value = value + chosen
    mixed_ref[0:NSP, :] = comp_ref[...] * value[NSP : NSP + 1] + value[0:NSP]
    level = level_ref[...].reshape(1, CHUNK)
    first, second = level == 0, level == 1
    z = dot(ops_ref[...], three(mixed_ref[...]))
    z = jnp.concatenate(
        [jnp.where(first, z[0:24], jnp.where(second, z[24:48], z[48:72])), z[72:104]], axis=0
    )
    source = jnp.concatenate([jnp.tanh(z), jnp.zeros((8, CHUNK), f32)], axis=0)
    z = dot(maps_ref[...], three(source))
    change = jnp.concatenate(
        [
            jnp.where(first, z[0:24], jnp.where(second, z[24:48], z[48:72])),
            jnp.where(level == 2, z[72:104], 0.0),
        ],
        axis=0,
    )
    updated_ref[...] = mixed_ref[0:NSP, :] + change[0:NSP]


def swap(x, axis, odd):
    count = lax.axis_size(axis)
    pairs = [(i, i + 1) for i in range(odd, count - 1, 2)]
    return lax.ppermute(x, axis, pairs + [(b, a) for a, b in pairs])


def whole(shape):
    return pl.BlockSpec(shape, lambda i: (0,) * len(shape))


def per_device(
    composition,
    particle_mass,
    particle_cell,
    particle_level,
    les_mean,
    mix_rate,
    rate_matrix,
    implicit_map,
):
    particles = composition.shape[1]
    grid = (particles // CHUNK,)
    columns = lambda rows: pl.BlockSpec((rows, CHUNK), lambda i: (0, i))
    line = pl.BlockSpec((CHUNK,), lambda i: (i,))
    sds = jax.ShapeDtypeStruct
    main, edge = pl.pallas_call(
        sums_kernel,
        grid=grid,
        out_shape=(sds((GROUPS * ROWS, 2 * CY), f32), sds((ROWS, 128), f32)),
        in_specs=[columns(NSP), line, columns(2), whole((NSP, CX, CY)), whole((CX, CY))],
        out_specs=(whole((GROUPS * ROWS, 2 * CY)), whole((ROWS, 128))),
        scratch_shapes=[pltpu.VMEM((ROWS, CHUNK), f32)],
        compiler_params=pltpu.CompilerParams(vmem_limit_bytes=32 << 20),
        name="cell_sums",
    )(composition, particle_mass, particle_cell, les_mean, mix_rate)
    edge_even = swap(edge, "gy", 0)
    edge_odd = swap(edge, "gy", 1)
    payload = sds((2 * ROWS + 8, 2 * CY), f32)
    even, odd = pl.pallas_call(
        pack_kernel,
        out_shape=(payload, payload),
        compiler_params=pltpu.CompilerParams(vmem_limit_bytes=32 << 20),
        name="pack",
    )(main, edge, edge_even, edge_odd)
    even_in = swap(even, "gx", 0)
    odd_in = swap(odd, "gx", 1)
    updated, means = pl.pallas_call(
        react_kernel,
        grid=grid,
        out_shape=(sds(composition.shape, f32), sds(les_mean.shape, f32)),
        in_specs=[whole(payload.shape)] * 4
        + [whole(rate_matrix.shape)] * 2
        + [columns(NSP), columns(2), line],
        out_specs=(columns(NSP), whole(les_mean.shape)),
        scratch_shapes=[
            pltpu.VMEM((GROUPS * ROWS, 2 * CY), f32),
            pltpu.VMEM((GROUPS * ROWS, 2 * CY), f32),
            pltpu.VMEM((ROWS, 128), bf16),
            pltpu.VMEM((104, 192), f32),
            pltpu.VMEM((104, 192), bf16),
            pltpu.VMEM((104, 192), bf16),
            pltpu.VMEM((64, CHUNK), f32),
        ],
        compiler_params=pltpu.CompilerParams(vmem_limit_bytes=32 << 20),
        name="gather_react",
    )(even, odd, even_in, odd_in, rate_matrix, implicit_map, composition, particle_cell, particle_level)
    return updated, means


def solution(mesh):
    placed = (
        P(None, ("gx", "gy")),
        P(("gx", "gy")),
        P(None, ("gx", "gy")),
        P(("gx", "gy")),
        P(None, "gx", "gy"),
        P("gx", "gy"),
        P(),
        P(),
    )
    return jax.shard_map(
        per_device,
        mesh=mesh,
        in_specs=placed,
        out_specs=(P(None, ("gx", "gy")), P(None, "gx", "gy")),
        check_vma=False,
    )
```

time: 267 us -> 38.5 us (0.14); the launches traced: 262 us -> 38.2 us
  other arithmetic: 108 us -> 0 us
  local copies, waits for them, and re-layouts: 81.9 us -> 4.68 us
  starting transfers between devices: 52.5 us -> 9.71 us
  Pallas kernels: 0 us -> 16.8 us
  matrix products: 13.4 us -> 0 us
    scatter-add x2 -> x0, other arithmetic: 101 us -> none  [the longest x1 56.8 us: per_device(): jnp.zeros((1, span_x * span_y), jnp.float32).at[:, ext_index]]
    gather x3 -> x0, local copies, waits for them, and re-layouts: 77.2 us -> none  [the longest x1 45.5 us: per_device(): jnp.take(ext_rate.reshape(span_x * span_y), ext_index, axis=0)]
    ppermute x16 -> x4, starting transfers between devices: 52.5 us -> 9.71 us  [swap(): return lax.ppermute(x, axis, pairs + [(b, a) for a, b in pairs])]
    pallas_call x0 -> x3, Pallas kernels: none -> 16.8 us  [the longest x1 9.03 us: per_device(): pl.pallas_call(react_kernel, grid=grid, out_shape=(sds(composition.shape,...]
    dot_general x6 -> x0, matrix products: 13.4 us -> none  [the longest x3 7.35 us: react_padded(): jnp.dot(implicit_map[tier_index], source, precision=lax.Precision.HIGHEST...]
    unnamed x18 -> x20, local copies, waits for them, and re-layouts: 0.04 us -> 4.68 us
    mul x1 -> x0, local copies, waits for them, and re-layouts: 2.76 us -> none  [per_device(): weighted = composition * particle_mass[None, :]]
    ppermute x16 -> x4, waiting for transfers between devices: 5.04 us -> 6.23 us  [swap(): return lax.ppermute(x, axis, pairs + [(b, a) for a, b in pairs])]
  transfers between devices with their start and end apart: 16 -> 4, of which waited for: 3 -> 3; matrix products, arithmetic and copies ran while one was open for 37% -> 0% of each run, Pallas kernels for 0% -> 0%
where the time goes in v1:
time: 38.5 us; the launch traced here: 38.2 us
  Pallas kernels  16.8 us (44%)
  starting transfers between devices  9.71 us (25%)
  waiting for transfers between devices  6.23 us (16%)
  local copies, waits for them, and re-layouts  4.68 us (12%)
  between operations  0.71 us (2%)
    ppermute x4, starting transfers between devices, swap(): return lax.ppermute(x, axis, pairs + [(b, a) for a, b in pairs])  9.71 us
    pallas_call x1, Pallas kernels, per_device(): pl.pallas_call(react_kernel, grid=grid, out_shape=(sds(composition.shape,...  9.03 us
    pallas_call x1, Pallas kernels, per_device(): pl.pallas_call(sums_kernel, grid=grid, out_shape=(sds((GROUPS * ROWS, 2 *...  7.59 us
    ppermute x4, waiting for transfers between devices, swap(): return lax.ppermute(x, axis, pairs + [(b, a) for a, b in pairs])  6.23 us
    unnamed x20, local copies, waits for them, and re-layouts  4.68 us
  transfers between devices with their start and end apart: 4, of which 3 were waited for; matrix products, arithmetic and copies ran while one was open for 0% of the time, Pallas kernels for 0%

profile of v1, /device:TPU:24, one launch (start us, length us, event | category | flops | bytes accessed | tf_op | source)
XLA Modules:
  0.0 38.2 jit_solution(2195774664866205030)
XLA Ops:
  0.6 0.0 copy-start
  0.6 1.5 %copy-done = f32[53,8192]{1,0:T(8,128)S(1)} copy-done((f32[53,8192]{1,0:T(8,128)S(1)}, f32[53,8192]{1,0:T(8,128)}, u32[]{:S(2)}) %copy-start) | copy-done | bytes 1736728
  2.1 0.0 copy-start.2
  2.1 0.8 %copy-done.2 = s32[2,8192]{1,0:T(2,128)S(1)} copy-done((s32[2,8192]{1,0:T(2,128)S(1)}, s32[2,8192]{1,0:T(2,128)}, u32[]{:S(2)}) %copy-start.2) | copy-done | bytes 65560
  3.0 0.0 copy-start.4
  3.0 0.9 %copy-done.4 = f32[53,4,128]{2,1,0:T(4,128)S(1)} copy-done((f32[53,4,128]{2,1,0:T(4,128)S(1)}, f32[53,4,128]{2,1,0:T(4,128)}, u32[]{:S(2)}) %copy-start.4) | copy-done | bytes 108568
  3.9 0.0 copy-start.7
  3.9 0.8 %copy-done.7 = f32[8192]{0:T(1024)S(1)} copy-done((f32[8192]{0:T(1024)S(1)}, f32[8192]{0:T(1024)}, u32[]{:S(2)}) %copy-start.7) | copy-done | bytes 32792
  4.6 0.0 copy-start.9
  4.6 0.7 %copy-done.9 = f32[4,128]{1,0:T(4,128)S(1)} copy-done((f32[4,128]{1,0:T(4,128)S(1)}, f32[4,128]{1,0:T(4,128)}, u32[]{:S(2)}) %copy-start.9) | copy-done | bytes 2072
  5.3 0.0 copy-start.1
  5.3 0.0 copy-start.3
  5.3 0.0 copy-start.5
  5.3 0.0 copy-start.6
  5.3 0.0 copy-start.8
  5.3 7.6 %cell_sums.1 = (f32[224,256]{1,0:T(8,128)S(1)}, f32[56,128]{1,0:T(8,128)S(1)}) custom-call(f32[53,8192]{1,0:T(8,128)S(1)} %copy-done, f32[8192]{0:T(1024)S(1)} %copy-done.7, s32[2,8192]{1,0:T(2,128)S(1)} %copy-done.2, f32[53,4,128]{2,1,0:T(4,128)S(1)} %copy-done.4, f32[4,128]{1,0:T(4,128)S(1)} %copy-done.9), custom_call_target="tpu_custom_call" | custom-call | tf_op jit(solution)/shard_map/cell_sums/pallas_call | solution.py:293
  12.9 0.7 %collective-permute-start.1 = (f32[56,128]{1,0:T(8,128)S(1)}, f32[56,128]{1,0:T(8,128)S(1)}, u32[]{:S(2)}, u32[]{:S(2)}) collective-permute-start(f32[56,128]{1,0:T(8,128)S(1)} %get-tuple-element.7.edge_ref), channel_id=1, source_target_pairs={{1,2},{3,4},{5,6},{2,1},{4,3},{6,5},{9,10},{11,12},{13,14},{10,9},... | collective-permute-start | bytes 86024 | tf_op jit(solution)/shard_map/ppermute | solution.py:271
  13.6 3.4 %collective-permute-start = (f32[56,128]{1,0:T(8,128)S(1)}, f32[56,128]{1,0:T(8,128)S(1)}, u32[]{:S(2)}, u32[]{:S(2)}) collective-permute-start(f32[56,128]{1,0:T(8,128)S(1)} %get-tuple-element.7.edge_ref), channel_id=1, source_target_pairs={{0,1},{2,3},{4,5},{6,7},{1,0},{3,2},{5,4},{7,6},{8,9},{10,11},{12,... | collective-permute-start | bytes 86024 | tf_op jit(solution)/shard_map/ppermute | solution.py:271
  17.0 0.0 collective-permute-done.1.odd_in_ref
  17.0 0.9 %collective-permute-done.even_in_ref = f32[56,128]{1,0:T(8,128)S(1)} collective-permute-done((f32[56,128]{1,0:T(8,128)S(1)}, f32[56,128]{1,0:T(8,128)S(1)}, u32[]{:S(2)}, u32[]{:S(2)}) %collective-permute-start) | collective-permute-done | bytes 28704 | tf_op jit(solution)/shard_map/ppermute | solution.py:271
  17.8 0.2 pack.1
  18.0 1.5 %collective-permute-start.2 = (f32[120,256]{1,0:T(8,128)S(1)}, f32[120,256]{1,0:T(8,128)S(1)}, u32[]{:S(2)}, u32[]{:S(2)}) collective-permute-start(f32[120,256]{1,0:T(8,128)S(1)} %get-tuple-element.8.even_ref), channel_id=1, source_target_pairs={{0,8},{16,24},{32,40},{48,56},{64,72},{80,88},{96,104},{112,120},{... | collective-permute-start | bytes 368648 | tf_op jit(solution)/shard_map/ppermute | solution.py:271
  19.6 4.2 %collective-permute-start.3 = (f32[120,256]{1,0:T(8,128)S(1)}, f32[120,256]{1,0:T(8,128)S(1)}, u32[]{:S(2)}, u32[]{:S(2)}) collective-permute-start(f32[120,256]{1,0:T(8,128)S(1)} %get-tuple-element.9.odd_ref), channel_id=1, source_target_pairs={{8,16},{24,32},{40,48},{56,64},{72,80},{88,96},{104,112},{16,8},{3... | collective-permute-start | bytes 368648 | tf_op jit(solution)/shard_map/ppermute | solution.py:271
  23.7 0.2 collective-permute-done.2.even_in_ref
  23.9 5.2 %collective-permute-done.3.odd_in_ref = f32[120,256]{1,0:T(8,128)S(1)} collective-permute-done((f32[120,256]{1,0:T(8,128)S(1)}, f32[120,256]{1,0:T(8,128)S(1)}, u32[]{:S(2)}, u32[]{:S(2)}) %collective-permute-start.3) | collective-permute-done | bytes 122912 | tf_op jit(solution)/shard_map/ppermute | solution.py:271
  29.1 0.0 copy-done.1
  29.1 0.0 copy-done.3
  29.1 0.0 copy-done.5
  29.1 0.0 copy-done.6
  29.1 0.0 copy-done.8
  29.1 9.0 %gather_react.1 = (f32[53,8192]{1,0:T(8,128)}, f32[53,4,128]{2,1,0:T(4,128)}) custom-call(f32[120,256]{1,0:T(8,128)S(1)} %get-tuple-element.8.even_ref, f32[120,256]{1,0:T(8,128)S(1)} %get-tuple-element.9.odd_ref, f32[120,256]{1,0:T(8,128)S(1)} %collective-permute-done.2.even_in_ref, f32[120,256]{1,0:T(8,128)S(1)} %collective-permute-done.3.odd_in_ref, ...), custom_call_target="tpu_custom_call" | custom-call | tf_op jit(solution)/shard_map/gather_react/pallas_call | solution.py:314
Async XLA Ops:
  0.6 1.5 %copy-start = (f32[53,8192]{1,0:T(8,128)S(1)}, f32[53,8192]{1,0:T(8,128)}, u32[]{:S(2)}) copy-start(f32[53,8192]{1,0:T(8,128)} %comp_ref.3) | copy-start | bytes 5210116
  2.1 0.8 %copy-start.2 = (s32[2,8192]{1,0:T(2,128)S(1)}, s32[2,8192]{1,0:T(2,128)}, u32[]{:S(2)}) copy-start(s32[2,8192]{1,0:T(2,128)} %cell_ref.3) | copy-start | bytes 196612
  3.0 0.9 %copy-start.4 = (f32[53,4,128]{2,1,0:T(4,128)S(1)}, f32[53,4,128]{2,1,0:T(4,128)}, u32[]{:S(2)}) copy-start(f32[53,4,128]{2,1,0:T(4,128)} %les_ref.1) | copy-start | bytes 325636
  3.9 0.8 %copy-start.7 = (f32[8192]{0:T(1024)S(1)}, f32[8192]{0:T(1024)}, u32[]{:S(2)}) copy-start(f32[8192]{0:T(1024)} %mass_ref.1) | copy-start | bytes 98308
  4.6 0.7 %copy-start.9 = (f32[4,128]{1,0:T(4,128)S(1)}, f32[4,128]{1,0:T(4,128)}, u32[]{:S(2)}) copy-start(f32[4,128]{1,0:T(4,128)} %rate_ref.2) | copy-start | bytes 6148
  5.3 23.8 %copy-start.1 = (f32[53,8192]{1,0:T(8,128)S(1)}, f32[53,8192]{1,0:T(8,128)}, u32[]{:S(2)}) copy-start(f32[53,8192]{1,0:T(8,128)} %comp_ref.3) | copy-start | bytes 5210116
  5.3 23.8 %copy-start.3 = (s32[2,8192]{1,0:T(2,128)S(1)}, s32[2,8192]{1,0:T(2,128)}, u32[]{:S(2)}) copy-start(s32[2,8192]{1,0:T(2,128)} %cell_ref.3) | copy-start | bytes 196612
  5.3 23.8 %copy-start.5 = (f32[3,53,53]{2,1,0:T(8,128)S(1)}, f32[3,53,53]{2,1,0:T(8,128)}, u32[]{:S(2)}) copy-start(f32[3,53,53]{2,1,0:T(8,128)} %rate_ref.3) | copy-start | bytes 101128
  5.3 23.8 %copy-start.6 = (f32[3,53,53]{2,1,0:T(8,128)S(1)}, f32[3,53,53]{2,1,0:T(8,128)}, u32[]{:S(2)}) copy-start(f32[3,53,53]{2,1,0:T(8,128)} %map_ref.1) | copy-start | bytes 101128
  5.3 23.8 %copy-start.8 = (s32[8192]{0:T(1024)S(1)}, s32[8192]{0:T(1024)}, u32[]{:S(2)}) copy-start(s32[8192]{0:T(1024)} %level_ref.1) | copy-start | bytes 98308
  12.9 4.0 %collective-permute-start.1 = (f32[56,128]{1,0:T(8,128)S(1)}, f32[56,128]{1,0:T(8,128)S(1)}, u32[]{:S(2)}, u32[]{:S(2)}) collective-permute-start(f32[56,128]{1,0:T(8,128)S(1)} %get-tuple-element.7.edge_ref), channel_id=1, source_target_pairs={{1,2},{3,4},{5,6},{2,1},{4,3},{6,5},{9,10},{11,12},{13,14},{10,9},... | collective-permute-start | bytes 86024 | tf_op jit(solution)/shard_map/ppermute | solution.py:271
  13.6 4.2 %collective-permute-start = (f32[56,128]{1,0:T(8,128)S(1)}, f32[56,128]{1,0:T(8,128)S(1)}, u32[]{:S(2)}, u32[]{:S(2)}) collective-permute-start(f32[56,128]{1,0:T(8,128)S(1)} %get-tuple-element.7.edge_ref), channel_id=1, source_target_pairs={{0,1},{2,3},{4,5},{6,7},{1,0},{3,2},{5,4},{7,6},{8,9},{10,11},{12,... | collective-permute-start | bytes 86024 | tf_op jit(solution)/shard_map/ppermute | solution.py:271
  18.0 5.9 %collective-permute-start.2 = (f32[120,256]{1,0:T(8,128)S(1)}, f32[120,256]{1,0:T(8,128)S(1)}, u32[]{:S(2)}, u32[]{:S(2)}) collective-permute-start(f32[120,256]{1,0:T(8,128)S(1)} %get-tuple-element.8.even_ref), channel_id=1, source_target_pairs={{0,8},{16,24},{32,40},{48,56},{64,72},{80,88},{96,104},{112,120},{... | collective-permute-start | bytes 368648 | tf_op jit(solution)/shard_map/ppermute | solution.py:271
  19.6 9.5 %collective-permute-start.3 = (f32[120,256]{1,0:T(8,128)S(1)}, f32[120,256]{1,0:T(8,128)S(1)}, u32[]{:S(2)}, u32[]{:S(2)}) collective-permute-start(f32[120,256]{1,0:T(8,128)S(1)} %get-tuple-element.9.odd_ref), channel_id=1, source_target_pairs={{8,16},{24,32},{40,48},{56,64},{72,80},{88,96},{104,112},{16,8},{3... | collective-permute-start | bytes 368648 | tf_op jit(solution)/shard_map/ppermute | solution.py:271

commit v2 on v1

v2 whole, which is shorter than its diff:
```python
import jax
import jax.numpy as jnp
from jax import lax
from jax.experimental import pallas as pl
from jax.experimental.pallas import tpu as pltpu
from jax.sharding import PartitionSpec as P

NS_LOW = 21
NS_MID = 24
NSP = 53
R = 2
CX = 4
CY = 128
ROWS = 56
GROUPS = 4
BANDS = GROUPS + 1
PART = 2048
CHUNK = 4096
VMEM = pltpu.CompilerParams(vmem_limit_bytes=40 << 20)

prior_weight = 16.0
chem_step = 0.5

f32 = jnp.float32
bf16 = jnp.bfloat16


def split(x):
    high = x.astype(bf16).astype(f32)
    return high, x - high


def stacked(x):
    high, low = split(x)
    return jnp.concatenate([high, low], axis=0).astype(bf16)


def local_cells(cells):
    local_x = cells[0:1, :] - (lax.axis_index("gx") * CX - R)
    local_y = cells[1:2, :] - (lax.axis_index("gy") * CY - R)
    return local_x, local_y


def edge_index(local_x, local_y):
    place = jnp.where(local_y < 2 * R, local_y, local_y - CY + 16)
    return (local_x >> 2) * 32 + (local_x & 3) * 4 + place


def band_and_index(local_x, local_y):
    inside = (local_y >= 2 * R) & (local_y < CY)
    band = jnp.where(inside, local_x >> 1, GROUPS)
    index = jnp.where(inside, (local_x & 1) * CY + local_y - R, edge_index(local_x, local_y))
    return band, index


def hot(index, count):
    cells = lax.broadcasted_iota(jnp.int32, (count, index.shape[1]), 0)
    return jnp.where(cells == index, 1.0, 0.0).astype(bf16)


def dot_nt(a, b):
    return lax.dot_general(a, b, (((1,), (1,)), ((), ())), preferred_element_type=f32)


def dot(a, b):
    return jnp.dot(a, b, preferred_element_type=f32)


def sums_kernel(
    comp_hbm, mass_hbm, cell_hbm, les_hbm, rate_hbm, main_ref, edge_ref, comp_ref,
    mass_ref, cell_ref, les_ref, rate_ref, w_ref, sems,
):
    particles = comp_ref.shape[1]
    parts = particles // PART
    pairs = [(les_hbm, les_ref), (rate_hbm, rate_ref), (cell_hbm, cell_ref), (mass_hbm, mass_ref)]
    small = len(pairs)
    for part in range(parts):
        at = pl.ds(part * PART, PART)
        pairs.append((comp_hbm.at[:, at], comp_ref.at[:, at]))
    copies = [pltpu.make_async_copy(src, dst, sems.at[i]) for i, (src, dst) in enumerate(pairs)]
    for copy in copies:
        copy.start()
    w_ref[...] = jnp.zeros_like(w_ref)
    main_ref[...] = jnp.zeros_like(main_ref)
    lane = lax.broadcasted_iota(jnp.int32, (ROWS, CY), 1)
    inner = (lane >= R) & (lane < CY - R)
    cells = CX * CY
    cell = lax.broadcasted_iota(jnp.int32, (1, cells), 1)
    band, index = band_and_index(cell // CY + R, cell % CY + R)
    place = hot(jnp.where(band == GROUPS, index, -1), 128)
    copies[0].wait()
    copies[1].wait()
    for x in range(CX):
        at = slice(x * CY, (x + 1) * CY)
        w_ref[0:NSP, at] = prior_weight * les_ref[:, x, :]
        w_ref[NSP : NSP + 1, at] = jnp.full((1, CY), prior_weight, f32)
        w_ref[NSP + 1 : NSP + 2, at] = rate_ref[x : x + 1, :]
        band, odd = divmod(x + R, 2)
        where = (slice(band * ROWS, (band + 1) * ROWS), slice(odd * CY, (odd + 1) * CY))
        main_ref[where] = jnp.where(inner, w_ref[:, at], 0.0)
    both = dot_nt(stacked(w_ref[:, 0:cells]), place)
    edge_ref[...] = both[0:ROWS] + both[ROWS:]
    w_ref[NSP : NSP + 2, :] = jnp.zeros((2, PART), f32)
    copies[2].wait()
    copies[3].wait()
    for part in range(parts):
        copies[small + part].wait()
        at = pl.ds(part * PART, PART)
        mass = mass_ref[at].reshape(1, PART)
        w_ref[0:NSP, :] = comp_ref[:, at] * mass
        w_ref[NSP : NSP + 1, :] = mass
        w = stacked(w_ref[...])
        band, index = band_and_index(*local_cells(cell_ref[:, at]))
        banded = [w * jnp.where(band == k, 1.0, 0.0).astype(bf16) for k in range(BANDS)]
        both = dot_nt(jnp.concatenate(banded, axis=0), hot(index, 2 * CY))
        for k in range(BANDS):
            start = 2 * ROWS * k
            sums = both[start : start + ROWS] + both[start + ROWS : start + 2 * ROWS]
            if k < GROUPS:
                main_ref[k * ROWS : (k + 1) * ROWS, :] += sums
            else:
                edge_ref[...] += sums[:, 0:128]


def pack_kernel(main_ref, edge_ref, even_in_ref, odd_in_ref, even_ref, odd_ref):
    odd_y = lax.axis_index("gy") % 2 == 1
    odd_x = lax.axis_index("gx") % 2 == 1
    even_in = even_in_ref[...]
    odd_in = odd_in_ref[...]
    row = lax.axis_index("gy")
    upper = jnp.where(row < lax.axis_size("gy") - 1, jnp.where(odd_y, odd_in, even_in), 0.0)
    lower = jnp.where(row > 0, jnp.where(odd_y, even_in, odd_in), 0.0)
    lane = lax.broadcasted_iota(jnp.int32, (ROWS, 128), 1)
    high = (lane & 16) != 0
    edge = edge_ref[...] + jnp.where(high, pltpu.roll(upper, 16, 1), pltpu.roll(lower, 112, 1))
    half = 2 * ROWS
    left, right = main_ref[0:half, :], main_ref[half:, :]
    even_ref[0:half, :] = jnp.where(odd_x, left, right)
    odd_ref[0:half, :] = jnp.where(odd_x, right, left)
    left_edge, right_edge = edge, pltpu.roll(edge, 96, 1)
    quarter = lane[0:8] >> 5
    for ref, part in (
        (even_ref, jnp.where(odd_x, left_edge, right_edge)),
        (odd_ref, jnp.where(odd_x, right_edge, left_edge)),
    ):
        for side in range(2):
            packed = jnp.zeros((8, 128), f32)
            for k in range(4):
                block = side * 4 + k
                if block < ROWS // 8:
                    rows = part[block * 8 : block * 8 + 8]
                    moved = pltpu.roll(rows, 32 * k, 1) if k else rows
                    packed = jnp.where(quarter == k, moved, packed)
            ref[half : half + 8, side * 128 : (side + 1) * 128] = packed


def table(total):
    rows = lax.broadcasted_iota(jnp.int32, total.shape, 0)
    mass = total[NSP : NSP + 1]
    mass = jnp.where(mass > 0.0, mass, 1.0)
    means = total / mass
    keep = jnp.exp(-total[NSP + 1 : NSP + 2])
    return means, jnp.where(rows < NSP, (1.0 - keep) * means, jnp.where(rows == NSP, keep, 0.0))


def unpacked(packed):
    lane = lax.broadcasted_iota(jnp.int32, (8, 128), 1)
    blocks = []
    for block in range(ROWS // 8):
        side, k = divmod(block, 4)
        rows = packed[:, side * 128 : (side + 1) * 128]
        rows = pltpu.roll(rows, 128 - 32 * k, 1) if k else rows
        blocks.append(jnp.where(lane < 32, rows, 0.0))
    return jnp.concatenate(blocks, axis=0)


def operator_rows(matrix_ref, full_ref, out_ref, scale):
    full_ref[...] = jnp.zeros_like(full_ref)
    start = 0
    for level, active in enumerate((NS_LOW, NS_MID, NSP)):
        rows = -(-active // 8) * 8
        count = min(rows, NSP)
        row = lax.broadcasted_iota(jnp.int32, (count, NSP), 0)
        col = lax.broadcasted_iota(jnp.int32, (count, NSP), 1)
        block = matrix_ref[level, 0:count, :] * scale
        high, low = split(jnp.where((row < active) & (col < active), block, 0.0))
        full_ref[start : start + count, 0:NSP] = high
        full_ref[start : start + count, 64 : 64 + NSP] = high
        full_ref[start : start + count, 128 : 128 + NSP] = low
        start += rows
    out_ref[...] = full_ref[...].astype(bf16)


def three(x):
    high, low = split(x)
    return jnp.concatenate([high, low, high], axis=0).astype(bf16)


def prepare_kernel(cell_ref, level_ref, rate_ref, map_ref, hot_ref, which_ref, ops_ref, maps_ref, full_ref):
    operator_rows(rate_ref, full_ref, ops_ref, 1.0)
    operator_rows(map_ref, full_ref, maps_ref, chem_step)
    particles = cell_ref.shape[1]
    which_ref[1:2, :] = level_ref[...].reshape(1, particles)

    def body(i, carry):
        at = pl.ds(pl.multiple_of(i * CHUNK, CHUNK), CHUNK)
        band, index = band_and_index(*local_cells(cell_ref[:, at]))
        which_ref[0:1, at] = band
        hot_ref[:, at] = hot(index, 2 * CY)
        return carry

    lax.fori_loop(0, particles // CHUNK, body, 0)


def react_kernel(
    even_ref, odd_ref, even_in_ref, odd_in_ref, ops_ref, maps_ref, hot_ref, which_ref, comp_ref,
    updated_hbm, means_hbm,
    means_ref, full_ref, cells_ref, mixed_ref, out_ref, sems,
):
    half = 2 * ROWS
    odd_x = lax.axis_index("gx") % 2 == 1
    even = even_ref[...] + even_in_ref[...]
    column = lax.axis_index("gx")
    at_end = (column == 0) | (column == lax.axis_size("gx") - 1)
    odd = odd_ref[...] + jnp.where(at_end, 0.0, odd_in_ref[...])
    left = jnp.where(odd_x, even, odd)
    right = jnp.where(odd_x, odd, even)
    edge = unpacked(left[half:, :]) + pltpu.roll(unpacked(right[half:, :]), 32, 1)
    lane = lax.broadcasted_iota(jnp.int32, (ROWS, 128), 1)
    edge_means, edge_table = table(edge)
    start = GROUPS * half
    full_ref[start:, 128:] = jnp.zeros((half, 128), f32)
    high, low = split(jnp.where(lane < 64, edge_table, 0.0))
    full_ref[start : start + ROWS, 0:128] = high
    full_ref[start + ROWS :, 0:128] = low
    high, low = split(edge_means)
    edge_means = jnp.where(lane < 64, high, pltpu.roll(low, 64, 1)).astype(bf16)
    row = lax.broadcasted_iota(jnp.int32, (128, CY), 0) & 63
    col = lax.broadcasted_iota(jnp.int32, (1, CY), 1)
    inner = (lane >= R) & (lane < CY - R)
    for group in range(GROUPS):
        source = left if group < 2 else right
        start = (group % 2) * ROWS
        means, cells = table(source[start : start + ROWS])
        high, low = split(cells)
        full_ref[group * half : group * half + ROWS, :] = high
        full_ref[group * half + ROWS : (group + 1) * half, :] = low
        if group in (1, 2):
            for odd_column in range(2):
                x = group * 2 + odd_column - R
                index = edge_index(jnp.full((1, CY), x + R, jnp.int32), col + R)
                placed = dot(edge_means, jnp.where(row == index, 1.0, 0.0).astype(bf16))
                own = jnp.where(inner, means[:, odd_column * CY : (odd_column + 1) * CY], placed)
                means_ref[:, x, :] = own[0:NSP]
    means_copy = pltpu.make_async_copy(means_ref, means_hbm, sems.at[0])
    means_copy.start()
    cells_ref[...] = full_ref[...].astype(bf16)
    mixed_ref[...] = jnp.zeros_like(mixed_ref)
    chunks = comp_ref.shape[1] // CHUNK

    def copy_of(chunk):
        at = pl.ds(chunk * CHUNK, CHUNK)
        return pltpu.make_async_copy(out_ref.at[:, at], updated_hbm.at[:, at], sems.at[1 + chunk])

    for chunk in range(chunks):
        at = pl.ds(chunk * CHUNK, CHUNK)
        gathered = dot(cells_ref[...], hot_ref[:, at])
        band = which_ref[0:1, at]
        chosen = gathered[0:half]
        for k in range(1, BANDS):
            chosen = jnp.where(band == k, gathered[k * half : (k + 1) * half], chosen)
        value = chosen[0:ROWS] + chosen[ROWS:]
        mixed_ref[0:NSP, :] = comp_ref[:, at] * value[NSP : NSP + 1] + value[0:NSP]
        level = which_ref[1:2, at]
        first, second = level == 0, level == 1
        z = dot(ops_ref[...], three(mixed_ref[...]))
        z = jnp.concatenate(
            [jnp.where(first, z[0:24], jnp.where(second, z[24:48], z[48:72])), z[72:104]], axis=0
        )
        source = jnp.concatenate([jnp.tanh(z), jnp.zeros((8, CHUNK), f32)], axis=0)
        z = dot(maps_ref[...], three(source))
        change = jnp.concatenate(
            [
                jnp.where(first, z[0:24], jnp.where(second, z[24:48], z[48:72])),
                jnp.where(level == 2, z[72:104], 0.0),
            ],
            axis=0,
        )
        out_ref[:, at] = mixed_ref[0:NSP, :] + change[0:NSP]
        copy_of(chunk).start()
    means_copy.wait()
    for chunk in range(chunks):
        copy_of(chunk).wait()


def swap(x, axis, odd):
    columns, rows = lax.axis_size("gx"), lax.axis_size("gy")

    def partner(i, j):
        at, count = (i, columns) if axis == "gx" else (j, rows)
        other = at + 1 if at % 2 == odd else at - 1
        if axis == "gx":
            return (other, j) if 0 <= other < count else (i, j ^ 1)
        return (i, other) if 0 <= other < count else (i ^ 1, j)

    pairs = []
    for i in range(columns):
        for j in range(rows):
            k, m = partner(i, j)
            pairs.append((i * rows + j, k * rows + m))
    return lax.ppermute(x, ("gx", "gy"), pairs)


def per_device(
    composition,
    particle_mass,
    particle_cell,
    particle_level,
    les_mean,
    mix_rate,
    rate_matrix,
    implicit_map,
):
    particles = composition.shape[1]
    parts = particles // PART
    sds = jax.ShapeDtypeStruct
    stay = lambda x: pltpu.with_memory_space_constraint(x, pltpu.HBM)
    hbm = pl.BlockSpec(memory_space=pltpu.HBM)
    vmem = pl.BlockSpec(memory_space=pltpu.VMEM)
    main, edge, local = pl.pallas_call(
        sums_kernel,
        out_shape=(
            sds((GROUPS * ROWS, 2 * CY), f32),
            sds((ROWS, 128), f32),
            sds(composition.shape, f32),
        ),
        in_specs=[hbm] * 5,
        out_specs=(vmem,) * 3,
        scratch_shapes=[
            pltpu.VMEM(particle_mass.shape, f32),
            pltpu.VMEM(particle_cell.shape, jnp.int32),
            pltpu.VMEM(les_mean.shape, f32),
            pltpu.VMEM(mix_rate.shape, f32),
            pltpu.VMEM((ROWS, PART), f32),
            pltpu.SemaphoreType.DMA((parts + 4,)),
        ],
        compiler_params=VMEM,
        name="cell_sums",
    )(*map(stay, (composition, particle_mass, particle_cell, les_mean, mix_rate)))
    edge_even = swap(edge, "gy", 0)
    edge_odd = swap(edge, "gy", 1)
    payload = sds((2 * ROWS + 8, 2 * CY), f32)
    even, odd = pl.pallas_call(
        pack_kernel,
        out_shape=(payload, payload),
        compiler_params=VMEM,
        name="pack",
    )(main, edge, edge_even, edge_odd)
    even_in = swap(even, "gx", 0)
    odd_in = swap(odd, "gx", 1)
    operator = sds((104, 192), bf16)
    places, which, ops, maps = pl.pallas_call(
        prepare_kernel,
        out_shape=(sds((2 * CY, particles), bf16), sds((2, particles), jnp.int32), operator, operator),
        in_specs=[vmem] * 4,
        out_specs=(vmem,) * 4,
        scratch_shapes=[pltpu.VMEM((104, 192), f32)],
        compiler_params=VMEM,
        cost_estimate=pl.CostEstimate(flops=1 << 22, bytes_accessed=8 << 20, transcendentals=0),
        name="prepare",
    )(particle_cell, particle_level, rate_matrix, implicit_map)
    return pl.pallas_call(
        react_kernel,
        out_shape=(sds(composition.shape, f32), sds(les_mean.shape, f32)),
        in_specs=[vmem] * 9,
        out_specs=(hbm, hbm),
        scratch_shapes=[
            pltpu.VMEM(les_mean.shape, f32),
            pltpu.VMEM((BANDS * 2 * ROWS, 2 * CY), f32),
            pltpu.VMEM((BANDS * 2 * ROWS, 2 * CY), bf16),
            pltpu.VMEM((64, CHUNK), f32),
            pltpu.VMEM(composition.shape, f32),
            pltpu.SemaphoreType.DMA((particles // CHUNK + 1,)),
        ],
        compiler_params=VMEM,
        name="gather_react",
    )(even, odd, even_in, odd_in, ops, maps, places, which, local)


def solution(mesh):
    placed = (
        P(None, ("gx", "gy")),
        P(("gx", "gy")),
        P(None, ("gx", "gy")),
        P(("gx", "gy")),
        P(None, "gx", "gy"),
        P("gx", "gy"),
        P(),
        P(),
    )
    return jax.shard_map(
        per_device,
        mesh=mesh,
        in_specs=placed,
        out_specs=(P(None, ("gx", "gy")), P(None, "gx", "gy")),
        check_vma=False,
    )
```

time: 38.5 us -> 25.5 us (0.66)
  local copies, waits for them, and re-layouts: 4.68 us -> 0.02 us
  Pallas kernels: 16.8 us -> 13 us
  starting transfers between devices: 9.71 us -> 5.91 us
  waiting for transfers between devices: 6.23 us -> 5.73 us
    unnamed x20 -> x8, local copies, waits for them, and re-layouts: 4.68 us -> 0.02 us
    pallas_call x2 -> x3, Pallas kernels: 16.6 us -> 12.8 us  [the longest x1 6.79 us: per_device(): pl.pallas_call(sums_kernel, out_shape=(sds((GROUPS * ROWS, 2 * CY), f32),...]
    ppermute x4, starting transfers between devices: 9.71 us -> 5.91 us  [swap(): return lax.ppermute(x, ('gx', 'gy'), pairs)]
    ppermute x4, waiting for transfers between devices: 6.23 us -> 5.73 us  [swap(): return lax.ppermute(x, ('gx', 'gy'), pairs)]
  transfers between devices with their start and end apart: 4 -> 4, of which waited for: 3 -> 3; matrix products, arithmetic and copies ran while one was open for 0% -> 0% of each run, Pallas kernels for 0% -> 3%
where the time goes in v2:
time: 25.5 us; the launch traced here: 25.4 us
  Pallas kernels  13 us (51%)
  starting transfers between devices  5.91 us (23%)
  waiting for transfers between devices  5.73 us (22%)
  between operations  0.69 us (3%)
    pallas_call x1, Pallas kernels, per_device(): pl.pallas_call(sums_kernel, out_shape=(sds((GROUPS * ROWS, 2 * CY), f32),...  6.79 us
    ppermute x4, starting transfers between devices, swap(): return lax.ppermute(x, ('gx', 'gy'), pairs)  5.91 us
    ppermute x4, waiting for transfers between devices, swap(): return lax.ppermute(x, ('gx', 'gy'), pairs)  5.73 us
    pallas_call x1, Pallas kernels, per_device(): pl.pallas_call(react_kernel, out_shape=(sds(composition.shape, f32), sds(...  5.12 us
    pallas_call x1, Pallas kernels, per_device(): pl.pallas_call(prepare_kernel, out_shape=(sds((2 * CY, particles), bf16),...  0.89 us
  transfers between devices with their start and end apart: 4, of which 3 were waited for; matrix products, arithmetic and copies ran while one was open for 0% of the time, Pallas kernels for 3%

profile of v2, /device:TPU:24, one launch (start us, length us, event | category | flops | bytes accessed | tf_op | source)
XLA Modules:
  0.0 25.4 jit_solution(17422461521464471170)
XLA Ops:
  0.6 0.0 copy-start
  0.6 0.0 copy-start.2
  0.7 0.0 copy-start.1
  0.7 0.0 copy-start.3
  0.7 6.8 %cell_sums.1 = (f32[224,256]{1,0:T(8,128)S(1)}, f32[56,128]{1,0:T(8,128)S(1)}, f32[53,8192]{1,0:T(8,128)S(1)}) custom-call(f32[53,8192]{1,0:T(8,128)} %comp_hbm.1, f32[8192]{0:T(1024)} %mass_hbm.1, s32[2,8192]{1,0:T(2,128)} %cell_ref.1, f32[53,4,128]{2,1,0:T(4,128)} %les_hbm.1, f32[4,128]{1,0:T(4,128)} %rate_hbm.1), custom_call_target="tpu_custom_call" | custom-call | tf_op jit(solution)/shard_map/cell_sums/pallas_call | solution.py:330
  7.5 1.6 %collective-permute-start.1 = (f32[56,128]{1,0:T(8,128)S(1)}, f32[56,128]{1,0:T(8,128)S(1)}, u32[]{:S(2)}, u32[]{:S(2)}) collective-permute-start(f32[56,128]{1,0:T(8,128)S(1)} %get-tuple-element.12.edge_ref), channel_id=1, source_target_pairs={{0,8},{1,2},{2,1},{3,4},{4,3},{5,6},{6,5},{7,15},{8,0},{9,10},{10,... | collective-permute-start | bytes 86024 | tf_op jit(solution)/shard_map/ppermute | solution.py:311
  9.0 0.5 %collective-permute-start = (f32[56,128]{1,0:T(8,128)S(1)}, f32[56,128]{1,0:T(8,128)S(1)}, u32[]{:S(2)}, u32[]{:S(2)}) collective-permute-start(f32[56,128]{1,0:T(8,128)S(1)} %get-tuple-element.12.edge_ref), channel_id=1, source_target_pairs={{0,1},{1,0},{2,3},{3,2},{4,5},{5,4},{6,7},{7,6},{8,9},{9,8},{10,11... | collective-permute-start | bytes 86024 | tf_op jit(solution)/shard_map/ppermute | solution.py:311
  9.6 1.8 %collective-permute-done.1.odd_in_ref = f32[56,128]{1,0:T(8,128)S(1)} collective-permute-done((f32[56,128]{1,0:T(8,128)S(1)}, f32[56,128]{1,0:T(8,128)S(1)}, u32[]{:S(2)}, u32[]{:S(2)}) %collective-permute-start.1) | collective-permute-done | bytes 28704 | tf_op jit(solution)/shard_map/ppermute | solution.py:311
  11.4 0.0 collective-permute-done.even_in_ref
  11.4 0.2 pack.1
  11.6 1.5 %collective-permute-start.2 = (f32[120,256]{1,0:T(8,128)S(1)}, f32[120,256]{1,0:T(8,128)S(1)}, u32[]{:S(2)}, u32[]{:S(2)}) collective-permute-start(f32[120,256]{1,0:T(8,128)S(1)} %get-tuple-element.13.even_ref), channel_id=1, source_target_pairs={{0,8},{1,9},{2,10},{3,11},{4,12},{5,13},{6,14},{7,15},{8,0},{9,1},... | collective-permute-start | bytes 368648 | tf_op jit(solution)/shard_map/ppermute | solution.py:311
  13.2 2.3 %collective-permute-start.3 = (f32[120,256]{1,0:T(8,128)S(1)}, f32[120,256]{1,0:T(8,128)S(1)}, u32[]{:S(2)}, u32[]{:S(2)}) collective-permute-start(f32[120,256]{1,0:T(8,128)S(1)} %get-tuple-element.14.odd_ref), channel_id=1, source_target_pairs={{0,1},{1,0},{2,3},{3,2},{4,5},{5,4},{6,7},{7,6},{8,16},{9,17},{10,... | collective-permute-start | bytes 368648 | tf_op jit(solution)/shard_map/ppermute | solution.py:311
  15.4 0.0 copy-done
  15.4 0.0 copy-done.2
  15.4 0.0 copy-done.1
  15.5 0.0 copy-done.3
  15.5 0.9 %prepare.1 = (bf16[256,8192]{1,0:T(8,128)(2,1)S(1)}, s32[2,8192]{1,0:T(2,128)S(1)}, bf16[104,192]{1,0:T(8,128)(2,1)S(1)}, bf16[104,192]{1,0:T(8,128)(2,1)S(1)}) custom-call(s32[2,8192]{1,0:T(2,128)S(1)} %copy-done, s32[8192]{0:T(1024)S(1)} %copy-done.3, f32[3,53,53]{2,1,0:T(8,128)S(1)} %copy-done.1, f32[3,53,53]{2,1,0:T(8,128)S(1)} %copy-done.2), custom_call_target="tpu_custom_call" | custom-call | flops 4194304 | bytes 8388608 | tf_op jit(solution)/shard_map/prepare/pallas_call | solution.py:362
  16.4 0.6 %collective-permute-done.2.even_in_ref = f32[120,256]{1,0:T(8,128)S(1)} collective-permute-done((f32[120,256]{1,0:T(8,128)S(1)}, f32[120,256]{1,0:T(8,128)S(1)}, u32[]{:S(2)}, u32[]{:S(2)}) %collective-permute-start.2) | collective-permute-done | bytes 122912 | tf_op jit(solution)/shard_map/ppermute | solution.py:311
  16.9 3.3 %collective-permute-done.3.odd_in_ref = f32[120,256]{1,0:T(8,128)S(1)} collective-permute-done((f32[120,256]{1,0:T(8,128)S(1)}, f32[120,256]{1,0:T(8,128)S(1)}, u32[]{:S(2)}, u32[]{:S(2)}) %collective-permute-start.3) | collective-permute-done | bytes 122912 | tf_op jit(solution)/shard_map/ppermute | solution.py:311
  20.2 5.1 %gather_react.1 = (f32[53,8192]{1,0:T(8,128)}, f32[53,4,128]{2,1,0:T(4,128)}) custom-call(f32[120,256]{1,0:T(8,128)S(1)} %get-tuple-element.13.even_ref, f32[120,256]{1,0:T(8,128)S(1)} %get-tuple-element.14.odd_ref, f32[120,256]{1,0:T(8,128)S(1)} %collective-permute-done.2.even_in_ref, f32[120,256]{1,0:T(8,128)S(1)} %collective-permute-done.3.odd_in_ref, ...), custom_call_target="tpu_custom_call" | custom-call | tf_op jit(solution)/shard_map/gather_react/pallas_call | solution.py:372
Async XLA Ops:
  0.6 14.8 %copy-start = (s32[2,8192]{1,0:T(2,128)S(1)}, s32[2,8192]{1,0:T(2,128)}, u32[]{:S(2)}) copy-start(s32[2,8192]{1,0:T(2,128)} %cell_ref.1) | copy-start | bytes 196612
  0.6 14.8 %copy-start.2 = (f32[3,53,53]{2,1,0:T(8,128)S(1)}, f32[3,53,53]{2,1,0:T(8,128)}, u32[]{:S(2)}) copy-start(f32[3,53,53]{2,1,0:T(8,128)} %map_ref.1) | copy-start | bytes 101128
  0.7 14.8 %copy-start.1 = (f32[3,53,53]{2,1,0:T(8,128)S(1)}, f32[3,53,53]{2,1,0:T(8,128)}, u32[]{:S(2)}) copy-start(f32[3,53,53]{2,1,0:T(8,128)} %rate_ref.1) | copy-start | bytes 101128
  0.7 14.8 %copy-start.3 = (s32[8192]{0:T(1024)S(1)}, s32[8192]{0:T(1024)}, u32[]{:S(2)}) copy-start(s32[8192]{0:T(1024)} %level_ref.1) | copy-start | bytes 98308
  7.5 4.0 %collective-permute-start.1 = (f32[56,128]{1,0:T(8,128)S(1)}, f32[56,128]{1,0:T(8,128)S(1)}, u32[]{:S(2)}, u32[]{:S(2)}) collective-permute-start(f32[56,128]{1,0:T(8,128)S(1)} %get-tuple-element.12.edge_ref), channel_id=1, source_target_pairs={{0,8},{1,2},{2,1},{3,4},{4,3},{5,6},{6,5},{7,15},{8,0},{9,10},{10,... | collective-permute-start | bytes 86024 | tf_op jit(solution)/shard_map/ppermute | solution.py:311
  9.0 2.4 %collective-permute-start = (f32[56,128]{1,0:T(8,128)S(1)}, f32[56,128]{1,0:T(8,128)S(1)}, u32[]{:S(2)}, u32[]{:S(2)}) collective-permute-start(f32[56,128]{1,0:T(8,128)S(1)} %get-tuple-element.12.edge_ref), channel_id=1, source_target_pairs={{0,1},{1,0},{2,3},{3,2},{4,5},{5,4},{6,7},{7,6},{8,9},{9,8},{10,11... | collective-permute-start | bytes 86024 | tf_op jit(solution)/shard_map/ppermute | solution.py:311
  11.6 5.3 %collective-permute-start.2 = (f32[120,256]{1,0:T(8,128)S(1)}, f32[120,256]{1,0:T(8,128)S(1)}, u32[]{:S(2)}, u32[]{:S(2)}) collective-permute-start(f32[120,256]{1,0:T(8,128)S(1)} %get-tuple-element.13.even_ref), channel_id=1, source_target_pairs={{0,8},{1,9},{2,10},{3,11},{4,12},{5,13},{6,14},{7,15},{8,0},{9,1},... | collective-permute-start | bytes 368648 | tf_op jit(solution)/shard_map/ppermute | solution.py:311
  13.2 7.1 %collective-permute-start.3 = (f32[120,256]{1,0:T(8,128)S(1)}, f32[120,256]{1,0:T(8,128)S(1)}, u32[]{:S(2)}, u32[]{:S(2)}) collective-permute-start(f32[120,256]{1,0:T(8,128)S(1)} %get-tuple-element.14.odd_ref), channel_id=1, source_target_pairs={{0,1},{1,0},{2,3},{3,2},{4,5},{5,4},{6,7},{7,6},{8,16},{9,17},{10,... | collective-permute-start | bytes 368648 | tf_op jit(solution)/shard_map/ppermute | solution.py:311

commit v3 on v2

--- a/solution.py
+++ b/solution.py
@@ -14,7 +14,7 @@
 ROWS = 56
 GROUPS = 4
 BANDS = GROUPS + 1
-PART = 2048
+ROWBLOCK = 8
 CHUNK = 4096
 VMEM = pltpu.CompilerParams(vmem_limit_bytes=40 << 20)
 
@@ -68,19 +68,17 @@
 
 def sums_kernel(
     comp_hbm, mass_hbm, cell_hbm, les_hbm, rate_hbm, main_ref, edge_ref, comp_ref,
-    mass_ref, cell_ref, les_ref, rate_ref, w_ref, sems,
+    mass_ref, cell_ref, les_ref, rate_ref, w_ref, hot_ref, sems,
 ):
     particles = comp_ref.shape[1]
-    parts = particles // PART
     pairs = [(les_hbm, les_ref), (rate_hbm, rate_ref), (cell_hbm, cell_ref), (mass_hbm, mass_ref)]
-    small = len(pairs)
-    for part in range(parts):
-        at = pl.ds(part * PART, PART)
-        pairs.append((comp_hbm.at[:, at], comp_ref.at[:, at]))
+    for start in range(0, NSP, ROWBLOCK):
+        at = pl.ds(start, min(ROWBLOCK, NSP - start))
+        pairs.append((comp_hbm.at[at], comp_ref.at[at]))
     copies = [pltpu.make_async_copy(src, dst, sems.at[i]) for i, (src, dst) in enumerate(pairs)]
     for copy in copies:
         copy.start()
-    w_ref[...] = jnp.zeros_like(w_ref)
+    w_ref[NSP:, :] = jnp.zeros((ROWS - NSP, particles), f32)
     main_ref[...] = jnp.zeros_like(main_ref)
     lane = lax.broadcasted_iota(jnp.int32, (ROWS, CY), 1)
     inner = (lane >= R) & (lane < CY - R)
@@ -99,30 +97,29 @@
         where = (slice(band * ROWS, (band + 1) * ROWS), slice(odd * CY, (odd + 1) * CY))
         main_ref[where] = jnp.where(inner, w_ref[:, at], 0.0)
     both = dot_nt(stacked(w_ref[:, 0:cells]), place)
-    edge_ref[...] = both[0:ROWS] + both[ROWS:]
-    w_ref[NSP : NSP + 2, :] = jnp.zeros((2, PART), f32)
-    copies[2].wait()
-    copies[3].wait()
-    for part in range(parts):
-        copies[small + part].wait()
-        at = pl.ds(part * PART, PART)
-        mass = mass_ref[at].reshape(1, PART)
-        w_ref[0:NSP, :] = comp_ref[:, at] * mass
-        w_ref[NSP : NSP + 1, :] = mass
-        w = stacked(w_ref[...])
-        band, index = band_and_index(*local_cells(cell_ref[:, at]))
-        banded = [w * jnp.where(band == k, 1.0, 0.0).astype(bf16) for k in range(BANDS)]
-        both = dot_nt(jnp.concatenate(banded, axis=0), hot(index, 2 * CY))
-        for k in range(BANDS):
-            start = 2 * ROWS * k
-            sums = both[start : start + ROWS] + both[start + ROWS : start + 2 * ROWS]
-            if k < GROUPS:
-                main_ref[k * ROWS : (k + 1) * ROWS, :] += sums
-            else:
-                edge_ref[...] += sums[:, 0:128]
-
-
-def pack_kernel(main_ref, edge_ref, even_in_ref, odd_in_ref, even_ref, odd_ref):
+    edge = both[0:ROWS] + both[ROWS:]
+    w_ref[NSP : NSP + 2, :] = jnp.zeros((2, particles), f32)
+    for copy in copies[2:]:
+        copy.wait()
+    mass = mass_ref[...].reshape(1, particles)
+    band, index = band_and_index(*local_cells(cell_ref[...]))
+    w_ref[0:NSP, :] = comp_ref[...] * mass
+    w_ref[NSP : NSP + 1, :] = mass
+    w = stacked(w_ref[...])
+    banded = [w * jnp.where(band == k, 1.0, 0.0).astype(bf16) for k in range(BANDS)]
+    both = dot_nt(jnp.concatenate(banded, axis=0), hot(index, 2 * CY))
+    for k in range(BANDS):
+        start = 2 * ROWS * k
+        sums = both[start : start + ROWS] + both[start + ROWS : start + 2 * ROWS]
+        if k < GROUPS:
+            main_ref[k * ROWS : (k + 1) * ROWS, :] += sums
+        else:
+            edge += sums[:, 0:128]
+    rest = pltpu.roll(jnp.concatenate([edge[32:], jnp.zeros((8, 128), f32)], axis=0), 64, 1)
+    edge_ref[...] = jnp.where(lane[0:32] < 64, edge[0:32], rest)
+
+
+def pack_kernel(main_ref, edge_ref, even_in_ref, odd_in_ref, odd_ref, even_ref):
     odd_y = lax.axis_index("gy") % 2 == 1
     odd_x = lax.axis_index("gx") % 2 == 1
     even_in = even_in_ref[...]
@@ -130,9 +127,10 @@
     row = lax.axis_index("gy")
     upper = jnp.where(row < lax.axis_size("gy") - 1, jnp.where(odd_y, odd_in, even_in), 0.0)
     lower = jnp.where(row > 0, jnp.where(odd_y, even_in, odd_in), 0.0)
-    lane = lax.broadcasted_iota(jnp.int32, (ROWS, 128), 1)
+    lane = lax.broadcasted_iota(jnp.int32, (32, 128), 1)
     high = (lane & 16) != 0
-    edge = edge_ref[...] + jnp.where(high, pltpu.roll(upper, 16, 1), pltpu.roll(lower, 112, 1))
+    both = edge_ref[...] + jnp.where(high, pltpu.roll(upper, 16, 1), pltpu.roll(lower, 112, 1))
+    edge = jnp.concatenate([both, pltpu.roll(both, 64, 1)[0 : ROWS - 32]], axis=0)
     half = 2 * ROWS
     left, right = main_ref[0:half, :], main_ref[half:, :]
     even_ref[0:half, :] = jnp.where(odd_x, left, right)
@@ -213,7 +211,7 @@
 
 
 def react_kernel(
-    even_ref, odd_ref, even_in_ref, odd_in_ref, ops_ref, maps_ref, hot_ref, which_ref, comp_ref,
+    odd_ref, even_ref, odd_in_ref, even_in_ref, ops_ref, maps_ref, hot_ref, which_ref, comp_ref,
     updated_hbm, means_hbm,
     means_ref, full_ref, cells_ref, mixed_ref, out_ref, sems,
 ):
@@ -322,7 +320,6 @@
     implicit_map,
 ):
     particles = composition.shape[1]
-    parts = particles // PART
     sds = jax.ShapeDtypeStruct
     stay = lambda x: pltpu.with_memory_space_constraint(x, pltpu.HBM)
     hbm = pl.BlockSpec(memory_space=pltpu.HBM)
@@ -331,7 +328,7 @@
         sums_kernel,
         out_shape=(
             sds((GROUPS * ROWS, 2 * CY), f32),
-            sds((ROWS, 128), f32),
+            sds((32, 128), f32),
             sds(composition.shape, f32),
         ),
         in_specs=[hbm] * 5,
@@ -341,8 +338,9 @@
             pltpu.VMEM(particle_cell.shape, jnp.int32),
             pltpu.VMEM(les_mean.shape, f32),
             pltpu.VMEM(mix_rate.shape, f32),
-            pltpu.VMEM((ROWS, PART), f32),
-            pltpu.SemaphoreType.DMA((parts + 4,)),
+            pltpu.VMEM((ROWS, particles), f32),
+            pltpu.VMEM((2 * CY, particles), bf16),
+            pltpu.SemaphoreType.DMA((4 + pl.cdiv(NSP, ROWBLOCK),)),
         ],
         compiler_params=VMEM,
         name="cell_sums",
@@ -350,14 +348,14 @@
     edge_even = swap(edge, "gy", 0)
     edge_odd = swap(edge, "gy", 1)
     payload = sds((2 * ROWS + 8, 2 * CY), f32)
-    even, odd = pl.pallas_call(
+    odd, even = pl.pallas_call(
         pack_kernel,
         out_shape=(payload, payload),
         compiler_params=VMEM,
         name="pack",
     )(main, edge, edge_even, edge_odd)
+    odd_in = swap(odd, "gx", 1)
     even_in = swap(even, "gx", 0)
-    odd_in = swap(odd, "gx", 1)
     operator = sds((104, 192), bf16)
     places, which, ops, maps = pl.pallas_call(
         prepare_kernel,
@@ -384,7 +382,7 @@
         ],
         compiler_params=VMEM,
         name="gather_react",
-    )(even, odd, even_in, odd_in, ops, maps, places, which, local)
+    )(odd, even, odd_in, even_in, ops, maps, places, which, local)
 
 
 def solution(mesh):

time: 25.5 us -> 22.4 us (0.88)
  Pallas kernels: 13 us -> 10.7 us
  starting transfers between devices: 5.91 us -> 5.12 us
    pallas_call x1, Pallas kernels: 6.79 us -> 4.39 us  [per_device(): pl.pallas_call(sums_kernel, out_shape=(sds((GROUPS * ROWS, 2 * CY), f32),...]
    ppermute x4, starting transfers between devices: 5.91 us -> 5.12 us  [swap(): return lax.ppermute(x, ('gx', 'gy'), pairs)]
  transfers between devices with their start and end apart: 4 -> 4, of which waited for: 3 -> 3; matrix products, arithmetic and copies ran while one was open for 0% -> 0% of each run, Pallas kernels for 3% -> 4%
where the time goes in v3:
time: 22.4 us; the launch traced here: 22.2 us
  Pallas kernels  10.7 us (48%)
  waiting for transfers between devices  5.72 us (26%)
  starting transfers between devices  5.12 us (23%)
  between operations  0.69 us (3%)
    ppermute x4, waiting for transfers between devices, swap(): return lax.ppermute(x, ('gx', 'gy'), pairs)  5.72 us
    pallas_call x1, Pallas kernels, per_device(): pl.pallas_call(react_kernel, out_shape=(sds(composition.shape, f32), sds(...  5.12 us
    ppermute x4, starting transfers between devices, swap(): return lax.ppermute(x, ('gx', 'gy'), pairs)  5.12 us
    pallas_call x1, Pallas kernels, per_device(): pl.pallas_call(sums_kernel, out_shape=(sds((GROUPS * ROWS, 2 * CY), f32),...  4.39 us
    pallas_call x1, Pallas kernels, per_device(): pl.pallas_call(prepare_kernel, out_shape=(sds((2 * CY, particles), bf16),...  0.89 us
  transfers between devices with their start and end apart: 4, of which 3 were waited for; matrix products, arithmetic and copies ran while one was open for 0% of the time, Pallas kernels for 4%

profile of v3, /device:TPU:24, one launch (start us, length us, event | category | flops | bytes accessed | tf_op | source)
XLA Modules:
  0.0 22.2 jit_solution(14225324771948365001)
XLA Ops:
  0.6 0.0 copy-start
  0.6 0.0 copy-start.2
  0.7 0.0 copy-start.1
  0.7 0.0 copy-start.3
  0.7 4.4 %cell_sums.1 = (f32[224,256]{1,0:T(8,128)S(1)}, f32[32,128]{1,0:T(8,128)S(1)}, f32[53,8192]{1,0:T(8,128)S(1)}) custom-call(f32[53,8192]{1,0:T(8,128)} %comp_hbm.1, f32[8192]{0:T(1024)} %mass_hbm.1, s32[2,8192]{1,0:T(2,128)} %cell_ref.1, f32[53,4,128]{2,1,0:T(4,128)} %les_hbm.1, f32[4,128]{1,0:T(4,128)} %rate_hbm.1), custom_call_target="tpu_custom_call" | custom-call | tf_op jit(solution)/shard_map/cell_sums/pallas_call | solution.py:327
  5.1 1.6 %collective-permute-start.1 = (f32[32,128]{1,0:T(8,128)S(1)}, f32[32,128]{1,0:T(8,128)S(1)}, u32[]{:S(2)}, u32[]{:S(2)}) collective-permute-start(f32[32,128]{1,0:T(8,128)S(1)} %get-tuple-element.12.edge_ref), channel_id=1, source_target_pairs={{0,8},{1,2},{2,1},{3,4},{4,3},{5,6},{6,5},{7,15},{8,0},{9,10},{10,... | collective-permute-start | bytes 49160 | tf_op jit(solution)/shard_map/ppermute | solution.py:309
  6.6 0.5 %collective-permute-start = (f32[32,128]{1,0:T(8,128)S(1)}, f32[32,128]{1,0:T(8,128)S(1)}, u32[]{:S(2)}, u32[]{:S(2)}) collective-permute-start(f32[32,128]{1,0:T(8,128)S(1)} %get-tuple-element.12.edge_ref), channel_id=1, source_target_pairs={{0,1},{1,0},{2,3},{3,2},{4,5},{5,4},{6,7},{7,6},{8,9},{9,8},{10,11... | collective-permute-start | bytes 49160 | tf_op jit(solution)/shard_map/ppermute | solution.py:309
  7.2 1.7 %collective-permute-done.1.odd_in_ref = f32[32,128]{1,0:T(8,128)S(1)} collective-permute-done((f32[32,128]{1,0:T(8,128)S(1)}, f32[32,128]{1,0:T(8,128)S(1)}, u32[]{:S(2)}, u32[]{:S(2)}) %collective-permute-start.1) | collective-permute-done | bytes 16416 | tf_op jit(solution)/shard_map/ppermute | solution.py:309
  8.9 0.0 collective-permute-done.even_in_ref
  8.9 0.3 %pack.1 = (f32[120,256]{1,0:T(8,128)S(1)}, f32[120,256]{1,0:T(8,128)S(1)}) custom-call(f32[224,256]{1,0:T(8,128)S(1)} %get-tuple-element.11.main_ref, f32[32,128]{1,0:T(8,128)S(1)} %get-tuple-element.12.edge_ref, f32[32,128]{1,0:T(8,128)S(1)} %collective-permute-done.even_in_ref, f32[32,128]{1,0:T(8,128)S(1)} %collective-permute-done.1.odd_in_ref), custom_call_target="tpu_custom_call" | custom-call | tf_op jit(solution)/shard_map/pack/pallas_call | solution.py:351
  9.2 3.0 %collective-permute-start.2 = (f32[120,256]{1,0:T(8,128)S(1)}, f32[120,256]{1,0:T(8,128)S(1)}, u32[]{:S(2)}, u32[]{:S(2)}) collective-permute-start(f32[120,256]{1,0:T(8,128)S(1)} %get-tuple-element.13.odd_ref), channel_id=1, source_target_pairs={{0,1},{1,0},{2,3},{3,2},{4,5},{5,4},{6,7},{7,6},{8,16},{9,17},{10,... | collective-permute-start | bytes 368648 | tf_op jit(solution)/shard_map/ppermute | solution.py:309
  12.1 0.0 collective-permute-start.3
  12.2 0.0 copy-done
  12.2 0.0 copy-done.2
  12.2 0.0 copy-done.1
  12.2 0.0 copy-done.3
  12.2 0.9 %prepare.1 = (bf16[256,8192]{1,0:T(8,128)(2,1)S(1)}, s32[2,8192]{1,0:T(2,128)S(1)}, bf16[104,192]{1,0:T(8,128)(2,1)S(1)}, bf16[104,192]{1,0:T(8,128)(2,1)S(1)}) custom-call(s32[2,8192]{1,0:T(2,128)S(1)} %copy-done, s32[8192]{0:T(1024)S(1)} %copy-done.3, f32[3,53,53]{2,1,0:T(8,128)S(1)} %copy-done.1, f32[3,53,53]{2,1,0:T(8,128)S(1)} %copy-done.2), custom_call_target="tpu_custom_call" | custom-call | flops 4194304 | bytes 8388608 | tf_op jit(solution)/shard_map/prepare/pallas_call | solution.py:360
  13.1 3.5 %collective-permute-done.2.odd_in_ref = f32[120,256]{1,0:T(8,128)S(1)} collective-permute-done((f32[120,256]{1,0:T(8,128)S(1)}, f32[120,256]{1,0:T(8,128)S(1)}, u32[]{:S(2)}, u32[]{:S(2)}) %collective-permute-start.2) | collective-permute-done | bytes 122912 | tf_op jit(solution)/shard_map/ppermute | solution.py:309
  16.6 0.5 %collective-permute-done.3.even_in_ref = f32[120,256]{1,0:T(8,128)S(1)} collective-permute-done((f32[120,256]{1,0:T(8,128)S(1)}, f32[120,256]{1,0:T(8,128)S(1)}, u32[]{:S(2)}, u32[]{:S(2)}) %collective-permute-start.3) | collective-permute-done | bytes 122912 | tf_op jit(solution)/shard_map/ppermute | solution.py:309
  17.1 5.1 %gather_react.1 = (f32[53,8192]{1,0:T(8,128)}, f32[53,4,128]{2,1,0:T(4,128)}) custom-call(f32[120,256]{1,0:T(8,128)S(1)} %get-tuple-element.13.odd_ref, f32[120,256]{1,0:T(8,128)S(1)} %get-tuple-element.14.even_ref, f32[120,256]{1,0:T(8,128)S(1)} %collective-permute-done.2.odd_in_ref, f32[120,256]{1,0:T(8,128)S(1)} %collective-permute-done.3.even_in_ref, ...), custom_call_target="tpu_custom_call" | custom-call | tf_op jit(solution)/shard_map/gather_react/pallas_call | solution.py:370
Async XLA Ops:
  0.6 11.6 %copy-start = (s32[2,8192]{1,0:T(2,128)S(1)}, s32[2,8192]{1,0:T(2,128)}, u32[]{:S(2)}) copy-start(s32[2,8192]{1,0:T(2,128)} %cell_ref.1) | copy-start | bytes 196612
  0.6 11.6 %copy-start.2 = (f32[3,53,53]{2,1,0:T(8,128)S(1)}, f32[3,53,53]{2,1,0:T(8,128)}, u32[]{:S(2)}) copy-start(f32[3,53,53]{2,1,0:T(8,128)} %map_ref.1) | copy-start | bytes 101128
  0.7 11.5 %copy-start.1 = (f32[3,53,53]{2,1,0:T(8,128)S(1)}, f32[3,53,53]{2,1,0:T(8,128)}, u32[]{:S(2)}) copy-start(f32[3,53,53]{2,1,0:T(8,128)} %rate_ref.1) | copy-start | bytes 101128
  0.7 11.5 %copy-start.3 = (s32[8192]{0:T(1024)S(1)}, s32[8192]{0:T(1024)}, u32[]{:S(2)}) copy-start(s32[8192]{0:T(1024)} %level_ref.1) | copy-start | bytes 98308
  5.1 3.8 %collective-permute-start.1 = (f32[32,128]{1,0:T(8,128)S(1)}, f32[32,128]{1,0:T(8,128)S(1)}, u32[]{:S(2)}, u32[]{:S(2)}) collective-permute-start(f32[32,128]{1,0:T(8,128)S(1)} %get-tuple-element.12.edge_ref), channel_id=1, source_target_pairs={{0,8},{1,2},{2,1},{3,4},{4,3},{5,6},{6,5},{7,15},{8,0},{9,10},{10,... | collective-permute-start | bytes 49160 | tf_op jit(solution)/shard_map/ppermute | solution.py:309
  6.6 2.3 %collective-permute-start = (f32[32,128]{1,0:T(8,128)S(1)}, f32[32,128]{1,0:T(8,128)S(1)}, u32[]{:S(2)}, u32[]{:S(2)}) collective-permute-start(f32[32,128]{1,0:T(8,128)S(1)} %get-tuple-element.12.edge_ref), channel_id=1, source_target_pairs={{0,1},{1,0},{2,3},{3,2},{4,5},{5,4},{6,7},{7,6},{8,9},{9,8},{10,11... | collective-permute-start | bytes 49160 | tf_op jit(solution)/shard_map/ppermute | solution.py:309
  9.2 7.4 %collective-permute-start.2 = (f32[120,256]{1,0:T(8,128)S(1)}, f32[120,256]{1,0:T(8,128)S(1)}, u32[]{:S(2)}, u32[]{:S(2)}) collective-permute-start(f32[120,256]{1,0:T(8,128)S(1)} %get-tuple-element.13.odd_ref), channel_id=1, source_target_pairs={{0,1},{1,0},{2,3},{3,2},{4,5},{5,4},{6,7},{7,6},{8,16},{9,17},{10,... | collective-permute-start | bytes 368648 | tf_op jit(solution)/shard_map/ppermute | solution.py:309
  12.1 5.0 %collective-permute-start.3 = (f32[120,256]{1,0:T(8,128)S(1)}, f32[120,256]{1,0:T(8,128)S(1)}, u32[]{:S(2)}, u32[]{:S(2)}) collective-permute-start(f32[120,256]{1,0:T(8,128)S(1)} %get-tuple-element.14.even_ref), channel_id=1, source_target_pairs={{0,8},{1,9},{2,10},{3,11},{4,12},{5,13},{6,14},{7,15},{8,0},{9,1},... | collective-permute-start | bytes 368648 | tf_op jit(solution)/shard_map/ppermute | solution.py:309

commit v4 on v3

--- a/solution.py
+++ b/solution.py
@@ -14,8 +14,10 @@
 ROWS = 56
 GROUPS = 4
 BANDS = GROUPS + 1
-ROWBLOCK = 8
+ROWBLOCK = 16
+EDGE = 64
 CHUNK = 4096
+CHUNKS = (5120, 3072)
 VMEM = pltpu.CompilerParams(vmem_limit_bytes=40 << 20)
 
 prior_weight = 16.0
@@ -58,6 +60,11 @@
     return jnp.where(cells == index, 1.0, 0.0).astype(bf16)
 
 
+def hot_pair(index, count):
+    cells = lax.broadcasted_iota(jnp.int32, (count, index.shape[1]), 0)
+    return jnp.where((cells == index[0:1]) | (cells == index[1:2]), 1.0, 0.0).astype(bf16)
+
+
 def dot_nt(a, b):
     return lax.dot_general(a, b, (((1,), (1,)), ((), ())), preferred_element_type=f32)
 
@@ -66,11 +73,28 @@
     return jnp.dot(a, b, preferred_element_type=f32)
 
 
-def sums_kernel(
-    comp_hbm, mass_hbm, cell_hbm, les_hbm, rate_hbm, main_ref, edge_ref, comp_ref,
-    mass_ref, cell_ref, les_ref, rate_ref, w_ref, hot_ref, sems,
+def own_cells(les_ref, rate_ref, cells_ref):
+    cells_ref[NSP:, :] = jnp.zeros((ROWS - NSP, CX * CY), f32)
+    for x in range(CX):
+        at = slice(x * CY, (x + 1) * CY)
+        cells_ref[0:NSP, at] = prior_weight * les_ref[:, x, :]
+        cells_ref[NSP : NSP + 1, at] = jnp.full((1, CY), prior_weight, f32)
+        cells_ref[NSP + 1 : NSP + 2, at] = rate_ref[x : x + 1, :]
+
+
+def weighted(comp_ref, mass_ref, w_ref):
+    particles = comp_ref.shape[1]
+    mass = mass_ref[...].reshape(1, particles)
+    w_ref[0:NSP, :] = comp_ref[...] * mass
+    w_ref[NSP : NSP + 1, :] = mass
+    w_ref[NSP + 1 :, :] = jnp.zeros((ROWS - NSP - 1, particles), f32)
+    return stacked(w_ref[...])
+
+
+def edge_kernel(
+    comp_hbm, mass_hbm, cell_hbm, les_hbm, rate_hbm, edge_ref, comp_ref,
+    mass_ref, cell_ref, les_ref, rate_ref, cells_ref, w_ref, sems,
 ):
-    particles = comp_ref.shape[1]
     pairs = [(les_hbm, les_ref), (rate_hbm, rate_ref), (cell_hbm, cell_ref), (mass_hbm, mass_ref)]
     for start in range(0, NSP, ROWBLOCK):
         at = pl.ds(start, min(ROWBLOCK, NSP - start))
@@ -78,45 +102,44 @@
     copies = [pltpu.make_async_copy(src, dst, sems.at[i]) for i, (src, dst) in enumerate(pairs)]
     for copy in copies:
         copy.start()
-    w_ref[NSP:, :] = jnp.zeros((ROWS - NSP, particles), f32)
-    main_ref[...] = jnp.zeros_like(main_ref)
-    lane = lax.broadcasted_iota(jnp.int32, (ROWS, CY), 1)
-    inner = (lane >= R) & (lane < CY - R)
     cells = CX * CY
     cell = lax.broadcasted_iota(jnp.int32, (1, cells), 1)
     band, index = band_and_index(cell // CY + R, cell % CY + R)
-    place = hot(jnp.where(band == GROUPS, index, -1), 128)
+    place = hot(jnp.where(band == GROUPS, index, -1), EDGE)
     copies[0].wait()
     copies[1].wait()
-    for x in range(CX):
-        at = slice(x * CY, (x + 1) * CY)
-        w_ref[0:NSP, at] = prior_weight * les_ref[:, x, :]
-        w_ref[NSP : NSP + 1, at] = jnp.full((1, CY), prior_weight, f32)
-        w_ref[NSP + 1 : NSP + 2, at] = rate_ref[x : x + 1, :]
-        band, odd = divmod(x + R, 2)
-        where = (slice(band * ROWS, (band + 1) * ROWS), slice(odd * CY, (odd + 1) * CY))
-        main_ref[where] = jnp.where(inner, w_ref[:, at], 0.0)
-    both = dot_nt(stacked(w_ref[:, 0:cells]), place)
-    edge = both[0:ROWS] + both[ROWS:]
-    w_ref[NSP : NSP + 2, :] = jnp.zeros((2, particles), f32)
+    own_cells(les_ref, rate_ref, cells_ref)
+    both = dot_nt(stacked(cells_ref[...]), place)
     for copy in copies[2:]:
         copy.wait()
-    mass = mass_ref[...].reshape(1, particles)
+    w = weighted(comp_ref, mass_ref, w_ref)
     band, index = band_and_index(*local_cells(cell_ref[...]))
-    w_ref[0:NSP, :] = comp_ref[...] * mass
-    w_ref[NSP : NSP + 1, :] = mass
-    w = stacked(w_ref[...])
-    banded = [w * jnp.where(band == k, 1.0, 0.0).astype(bf16) for k in range(BANDS)]
+    both += dot_nt(w, hot(jnp.where(band == GROUPS, index, -1), EDGE))
+    edge = both[0:ROWS] + both[ROWS:]
+    if EDGE < 128:
+        edge = jnp.concatenate([edge, jnp.zeros((ROWS, 128 - EDGE), f32)], axis=1)
+    lane = lax.broadcasted_iota(jnp.int32, (32, 128), 1)
+    rest = pltpu.roll(jnp.concatenate([edge[32:], jnp.zeros((8, 128), f32)], axis=0), 64, 1)
+    edge_ref[...] = jnp.where(lane < 64, edge[0:32], rest)
+
+
+def main_kernel(comp_ref, mass_ref, cell_ref, les_ref, rate_ref, main_ref, cells_ref, w_ref):
+    own_cells(les_ref, rate_ref, cells_ref)
+    w = weighted(comp_ref, mass_ref, w_ref)
+    band, index = band_and_index(*local_cells(cell_ref[...]))
+    banded = [w * jnp.where(band == k, 1.0, 0.0).astype(bf16) for k in range(GROUPS)]
     both = dot_nt(jnp.concatenate(banded, axis=0), hot(index, 2 * CY))
-    for k in range(BANDS):
+    lane = lax.broadcasted_iota(jnp.int32, (ROWS, CY), 1)
+    inner = (lane >= R) & (lane < CY - R)
+    for k in range(GROUPS):
         start = 2 * ROWS * k
         sums = both[start : start + ROWS] + both[start + ROWS : start + 2 * ROWS]
-        if k < GROUPS:
-            main_ref[k * ROWS : (k + 1) * ROWS, :] += sums
-        else:
-            edge += sums[:, 0:128]
-    rest = pltpu.roll(jnp.concatenate([edge[32:], jnp.zeros((8, 128), f32)], axis=0), 64, 1)
-    edge_ref[...] = jnp.where(lane[0:32] < 64, edge[0:32], rest)
+        for odd in range(2):
+            part = sums[:, odd * CY : (odd + 1) * CY]
+            x = 2 * k + odd - R
+            if 0 <= x < CX:
+                part = part + jnp.where(inner, cells_ref[:, x * CY : (x + 1) * CY], 0.0)
+            main_ref[k * ROWS : (k + 1) * ROWS, odd * CY : (odd + 1) * CY] = part
 
 
 def pack_kernel(main_ref, edge_ref, even_in_ref, odd_in_ref, odd_ref, even_ref):
@@ -190,8 +213,9 @@
 
 
 def three(x):
-    high, low = split(x)
-    return jnp.concatenate([high, low, high], axis=0).astype(bf16)
+    high = x.astype(bf16)
+    low = (x - high.astype(f32)).astype(bf16)
+    return jnp.concatenate([high, low, high], axis=0)
 
 
 def prepare_kernel(cell_ref, level_ref, rate_ref, map_ref, hot_ref, which_ref, ops_ref, maps_ref, full_ref):
@@ -204,7 +228,8 @@
         at = pl.ds(pl.multiple_of(i * CHUNK, CHUNK), CHUNK)
         band, index = band_and_index(*local_cells(cell_ref[:, at]))
         which_ref[0:1, at] = band
-        hot_ref[:, at] = hot(index, 2 * CY)
+        index = jnp.concatenate([index, jnp.where(band == GROUPS, index + 64, index)], axis=0)
+        hot_ref[:, at] = hot_pair(index, 2 * CY)
         return carry
 
     lax.fori_loop(0, particles // CHUNK, body, 0)
@@ -227,10 +252,9 @@
     lane = lax.broadcasted_iota(jnp.int32, (ROWS, 128), 1)
     edge_means, edge_table = table(edge)
     start = GROUPS * half
-    full_ref[start:, 128:] = jnp.zeros((half, 128), f32)
-    high, low = split(jnp.where(lane < 64, edge_table, 0.0))
-    full_ref[start : start + ROWS, 0:128] = high
-    full_ref[start + ROWS :, 0:128] = low
+    full_ref[start:, 128:] = jnp.zeros((ROWS, 128), f32)
+    high, low = split(edge_table)
+    full_ref[start:, 0:128] = jnp.where(lane < 64, high, pltpu.roll(low, 64, 1))
     high, low = split(edge_means)
     edge_means = jnp.where(lane < 64, high, pltpu.roll(low, 64, 1)).astype(bf16)
     row = lax.broadcasted_iota(jnp.int32, (128, CY), 0) & 63
@@ -254,28 +278,29 @@
     means_copy.start()
     cells_ref[...] = full_ref[...].astype(bf16)
     mixed_ref[...] = jnp.zeros_like(mixed_ref)
-    chunks = comp_ref.shape[1] // CHUNK
+    chunks = len(CHUNKS)
 
     def copy_of(chunk):
-        at = pl.ds(chunk * CHUNK, CHUNK)
+        at = pl.ds(sum(CHUNKS[:chunk]), CHUNKS[chunk])
         return pltpu.make_async_copy(out_ref.at[:, at], updated_hbm.at[:, at], sems.at[1 + chunk])
 
     for chunk in range(chunks):
-        at = pl.ds(chunk * CHUNK, CHUNK)
+        width = CHUNKS[chunk]
+        at = pl.ds(sum(CHUNKS[:chunk]), width)
         gathered = dot(cells_ref[...], hot_ref[:, at])
         band = which_ref[0:1, at]
         chosen = gathered[0:half]
-        for k in range(1, BANDS):
+        for k in range(1, GROUPS):
             chosen = jnp.where(band == k, gathered[k * half : (k + 1) * half], chosen)
-        value = chosen[0:ROWS] + chosen[ROWS:]
-        mixed_ref[0:NSP, :] = comp_ref[:, at] * value[NSP : NSP + 1] + value[0:NSP]
+        value = jnp.where(band == GROUPS, gathered[GROUPS * half :], chosen[0:ROWS] + chosen[ROWS:])
+        mixed_ref[0:NSP, 0:width] = comp_ref[:, at] * value[NSP : NSP + 1] + value[0:NSP]
         level = which_ref[1:2, at]
         first, second = level == 0, level == 1
-        z = dot(ops_ref[...], three(mixed_ref[...]))
+        z = dot(ops_ref[...], three(mixed_ref[:, 0:width]))
         z = jnp.concatenate(
             [jnp.where(first, z[0:24], jnp.where(second, z[24:48], z[48:72])), z[72:104]], axis=0
         )
-        source = jnp.concatenate([jnp.tanh(z), jnp.zeros((8, CHUNK), f32)], axis=0)
+        source = jnp.concatenate([jnp.tanh(z), jnp.zeros((8, width), f32)], axis=0)
         z = dot(maps_ref[...], three(source))
         change = jnp.concatenate(
             [
@@ -284,7 +309,7 @@
             ],
             axis=0,
         )
-        out_ref[:, at] = mixed_ref[0:NSP, :] + change[0:NSP]
+        out_ref[:, at] = mixed_ref[0:NSP, 0:width] + change[0:NSP]
         copy_of(chunk).start()
     means_copy.wait()
     for chunk in range(chunks):
@@ -324,27 +349,34 @@
     stay = lambda x: pltpu.with_memory_space_constraint(x, pltpu.HBM)
     hbm = pl.BlockSpec(memory_space=pltpu.HBM)
     vmem = pl.BlockSpec(memory_space=pltpu.VMEM)
-    main, edge, local = pl.pallas_call(
-        sums_kernel,
-        out_shape=(
-            sds((GROUPS * ROWS, 2 * CY), f32),
-            sds((32, 128), f32),
-            sds(composition.shape, f32),
-        ),
+    prior = pltpu.VMEM((ROWS, CX * CY), f32)
+    edge, local = pl.pallas_call(
+        edge_kernel,
+        out_shape=(sds((32, 128), f32), sds(composition.shape, f32)),
         in_specs=[hbm] * 5,
-        out_specs=(vmem,) * 3,
+        out_specs=(vmem, vmem),
         scratch_shapes=[
             pltpu.VMEM(particle_mass.shape, f32),
             pltpu.VMEM(particle_cell.shape, jnp.int32),
             pltpu.VMEM(les_mean.shape, f32),
             pltpu.VMEM(mix_rate.shape, f32),
+            prior,
             pltpu.VMEM((ROWS, particles), f32),
-            pltpu.VMEM((2 * CY, particles), bf16),
             pltpu.SemaphoreType.DMA((4 + pl.cdiv(NSP, ROWBLOCK),)),
         ],
         compiler_params=VMEM,
+        name="edge_sums",
+    )(*map(stay, (composition, particle_mass, particle_cell, les_mean, mix_rate)))
+    main = pl.pallas_call(
+        main_kernel,
+        out_shape=sds((GROUPS * ROWS, 2 * CY), f32),
+        in_specs=[vmem] * 5,
+        out_specs=vmem,
+        scratch_shapes=[prior, pltpu.VMEM((ROWS, particles), f32)],
+        compiler_params=VMEM,
+        cost_estimate=pl.CostEstimate(flops=1 << 32, bytes_accessed=8 << 20, transcendentals=0),
         name="cell_sums",
-    )(*map(stay, (composition, particle_mass, particle_cell, les_mean, mix_rate)))
+    )(local, particle_mass, particle_cell, les_mean, mix_rate)
     edge_even = swap(edge, "gy", 0)
     edge_odd = swap(edge, "gy", 1)
     payload = sds((2 * ROWS + 8, 2 * CY), f32)
@@ -374,11 +406,11 @@
         out_specs=(hbm, hbm),
         scratch_shapes=[
             pltpu.VMEM(les_mean.shape, f32),
-            pltpu.VMEM((BANDS * 2 * ROWS, 2 * CY), f32),
-            pltpu.VMEM((BANDS * 2 * ROWS, 2 * CY), bf16),
-            pltpu.VMEM((64, CHUNK), f32),
+            pltpu.VMEM(((BANDS + GROUPS) * ROWS, 2 * CY), f32),
+            pltpu.VMEM(((BANDS + GROUPS) * ROWS, 2 * CY), bf16),
+            pltpu.VMEM((64, max(CHUNKS)), f32),
             pltpu.VMEM(composition.shape, f32),
-            pltpu.SemaphoreType.DMA((particles // CHUNK + 1,)),
+            pltpu.SemaphoreType.DMA((len(CHUNKS) + 1,)),
         ],
         compiler_params=VMEM,
         name="gather_react",

time: 22.4 us -> 20.6 us (0.920)
  waiting for transfers between devices: 5.72 us -> 3.5 us
  Pallas kernels: 10.7 us -> 11.1 us
    ppermute x4, waiting for transfers between devices: 5.72 us -> 3.5 us  [swap(): return lax.ppermute(x, ('gx', 'gy'), pairs)]
    pallas_call x1, Pallas kernels: 0.89 us -> 1.41 us  [per_device(): pl.pallas_call(prepare_kernel, out_shape=(sds((2 * CY, particles), bf16),...]
    pallas_call x1, Pallas kernels: 5.12 us -> 4.78 us  [per_device(): pl.pallas_call(react_kernel, out_shape=(sds(composition.shape, f32), sds(...]
    pallas_call x1 -> x2, Pallas kernels: 4.39 us -> 4.61 us  [the longest x1 2.47 us: per_device(): pl.pallas_call(edge_kernel, out_shape=(sds((32, 128), f32), sds(compositi...]
  transfers between devices with their start and end apart: 4 -> 4, of which waited for: 3 -> 2; matrix products, arithmetic and copies ran while one was open for 0% -> 0% of each run, Pallas kernels for 4% -> 17%
where the time goes in v4:
time: 20.6 us; the launch traced here: 20.5 us
  Pallas kernels  11.1 us (54%)
  starting transfers between devices  5.13 us (25%)
  waiting for transfers between devices  3.5 us (17%)
  between operations  0.73 us (4%)
    ppermute x4, starting transfers between devices, swap(): return lax.ppermute(x, ('gx', 'gy'), pairs)  5.13 us
    pallas_call x1, Pallas kernels, per_device(): pl.pallas_call(react_kernel, out_shape=(sds(composition.shape, f32), sds(...  4.78 us
    ppermute x4, waiting for transfers between devices, swap(): return lax.ppermute(x, ('gx', 'gy'), pairs)  3.5 us
    pallas_call x1, Pallas kernels, per_device(): pl.pallas_call(edge_kernel, out_shape=(sds((32, 128), f32), sds(compositi...  2.47 us
    pallas_call x1, Pallas kernels, per_device(): pl.pallas_call(main_kernel, out_shape=sds((GROUPS * ROWS, 2 * CY), f32),...  2.15 us
    pallas_call x1, Pallas kernels, per_device(): pl.pallas_call(prepare_kernel, out_shape=(sds((2 * CY, particles), bf16),...  1.41 us
  transfers between devices with their start and end apart: 4, of which 2 were waited for; matrix products, arithmetic and copies ran while one was open for 0% of the time, Pallas kernels for 17%

profile of v4, /device:TPU:24, one launch (start us, length us, event | category | flops | bytes accessed | tf_op | source)
XLA Modules:
  0.0 20.5 jit_solution(5517121616577055504)
XLA Ops:
  0.6 0.0 copy-start
  0.6 0.0 copy-start.6
  0.7 0.0 copy-start.1
  0.7 0.0 copy-start.4
  0.7 2.5 %edge_sums.1 = (f32[32,128]{1,0:T(8,128)S(1)}, f32[53,8192]{1,0:T(8,128)S(1)}) custom-call(f32[53,8192]{1,0:T(8,128)} %comp_hbm.1, f32[8192]{0:T(1024)} %mass_ref.1, s32[2,8192]{1,0:T(2,128)} %cell_ref.3, f32[53,4,128]{2,1,0:T(4,128)} %les_ref.1, f32[4,128]{1,0:T(4,128)} %rate_ref.2), custom_call_target="tpu_custom_call" | custom-call | tf_op jit(solution)/shard_map/edge_sums/pallas_call | solution.py:353
  3.1 1.6 %collective-permute-start.1 = (f32[32,128]{1,0:T(8,128)S(1)}, f32[32,128]{1,0:T(8,128)S(1)}, u32[]{:S(2)}, u32[]{:S(2)}) collective-permute-start(f32[32,128]{1,0:T(8,128)S(1)} %get-tuple-element.11.edge_ref), channel_id=1, source_target_pairs={{0,8},{1,2},{2,1},{3,4},{4,3},{5,6},{6,5},{7,15},{8,0},{9,10},{10,... | collective-permute-start | bytes 49160 | tf_op jit(solution)/shard_map/ppermute | solution.py:334
  4.7 0.5 %collective-permute-start = (f32[32,128]{1,0:T(8,128)S(1)}, f32[32,128]{1,0:T(8,128)S(1)}, u32[]{:S(2)}, u32[]{:S(2)}) collective-permute-start(f32[32,128]{1,0:T(8,128)S(1)} %get-tuple-element.11.edge_ref), channel_id=1, source_target_pairs={{0,1},{1,0},{2,3},{3,2},{4,5},{5,4},{6,7},{7,6},{8,9},{9,8},{10,11... | collective-permute-start | bytes 49160 | tf_op jit(solution)/shard_map/ppermute | solution.py:334
  5.3 0.0 copy-done
  5.3 0.0 copy-done.6
  5.3 0.0 copy-done.1
  5.3 0.0 copy-done.4
  5.3 0.0 copy-start.2
  5.3 0.0 copy-start.3
  5.3 0.0 copy-start.5
  5.3 2.1 %cell_sums.1.main_ref = f32[224,256]{1,0:T(8,128)S(1)} custom-call(f32[53,8192]{1,0:T(8,128)S(1)} %get-tuple-element.10.comp_ref, f32[8192]{0:T(1024)S(1)} %copy-done.4, s32[2,8192]{1,0:T(2,128)S(1)} %copy-done, f32[53,4,128]{2,1,0:T(4,128)S(1)} %copy-done.1, f32[4,128]{1,0:T(4,128)S(1)} %copy-done.6), custom_call_target="tpu_custom_call" | custom-call | flops 4294967296 | bytes 8388608 | tf_op jit(solution)/shard_map/cell_sums/pallas_call | solution.py:370
  7.5 0.0 collective-permute-done.1.odd_in_ref
  7.5 0.0 collective-permute-done.even_in_ref
  7.5 0.3 %pack.1 = (f32[120,256]{1,0:T(8,128)S(1)}, f32[120,256]{1,0:T(8,128)S(1)}) custom-call(f32[224,256]{1,0:T(8,128)S(1)} %cell_sums.1.main_ref, f32[32,128]{1,0:T(8,128)S(1)} %get-tuple-element.11.edge_ref, f32[32,128]{1,0:T(8,128)S(1)} %collective-permute-done.even_in_ref, f32[32,128]{1,0:T(8,128)S(1)} %collective-permute-done.1.odd_in_ref), custom_call_target="tpu_custom_call" | custom-call | tf_op jit(solution)/shard_map/pack/pallas_call | solution.py:383
  7.8 3.0 %collective-permute-start.2 = (f32[120,256]{1,0:T(8,128)S(1)}, f32[120,256]{1,0:T(8,128)S(1)}, u32[]{:S(2)}, u32[]{:S(2)}) collective-permute-start(f32[120,256]{1,0:T(8,128)S(1)} %get-tuple-element.12.odd_ref), channel_id=1, source_target_pairs={{0,1},{1,0},{2,3},{3,2},{4,5},{5,4},{6,7},{7,6},{8,16},{9,17},{10,... | collective-permute-start | bytes 368648 | tf_op jit(solution)/shard_map/ppermute | solution.py:334
  10.7 0.0 collective-permute-start.3
  10.8 0.0 copy-done.2
  10.8 0.0 copy-done.3
  10.8 0.0 copy-done.5
  10.8 1.4 %prepare.1 = (bf16[256,8192]{1,0:T(8,128)(2,1)S(1)}, s32[2,8192]{1,0:T(2,128)S(1)}, bf16[104,192]{1,0:T(8,128)(2,1)S(1)}, bf16[104,192]{1,0:T(8,128)(2,1)S(1)}) custom-call(s32[2,8192]{1,0:T(2,128)S(1)} %copy-done, s32[8192]{0:T(1024)S(1)} %copy-done.5, f32[3,53,53]{2,1,0:T(8,128)S(1)} %copy-done.2, f32[3,53,53]{2,1,0:T(8,128)S(1)} %copy-done.3), custom_call_target="tpu_custom_call" | custom-call | flops 4194304 | bytes 8388608 | tf_op jit(solution)/shard_map/prepare/pallas_call | solution.py:392
  12.2 2.9 %collective-permute-done.2.odd_in_ref = f32[120,256]{1,0:T(8,128)S(1)} collective-permute-done((f32[120,256]{1,0:T(8,128)S(1)}, f32[120,256]{1,0:T(8,128)S(1)}, u32[]{:S(2)}, u32[]{:S(2)}) %collective-permute-start.2) | collective-permute-done | bytes 122912 | tf_op jit(solution)/shard_map/ppermute | solution.py:334
  15.2 0.5 %collective-permute-done.3.even_in_ref = f32[120,256]{1,0:T(8,128)S(1)} collective-permute-done((f32[120,256]{1,0:T(8,128)S(1)}, f32[120,256]{1,0:T(8,128)S(1)}, u32[]{:S(2)}, u32[]{:S(2)}) %collective-permute-start.3) | collective-permute-done | bytes 122912 | tf_op jit(solution)/shard_map/ppermute | solution.py:334
  15.7 4.8 %gather_react.1 = (f32[53,8192]{1,0:T(8,128)}, f32[53,4,128]{2,1,0:T(4,128)}) custom-call(f32[120,256]{1,0:T(8,128)S(1)} %get-tuple-element.12.odd_ref, f32[120,256]{1,0:T(8,128)S(1)} %get-tuple-element.13.even_ref, f32[120,256]{1,0:T(8,128)S(1)} %collective-permute-done.2.odd_in_ref, f32[120,256]{1,0:T(8,128)S(1)} %collective-permute-done.3.even_in_ref, ...), custom_call_target="tpu_custom_call" | custom-call | tf_op jit(solution)/shard_map/gather_react/pallas_call | solution.py:402
Async XLA Ops:
  0.6 4.6 %copy-start = (s32[2,8192]{1,0:T(2,128)S(1)}, s32[2,8192]{1,0:T(2,128)}, u32[]{:S(2)}) copy-start(s32[2,8192]{1,0:T(2,128)} %cell_ref.3) | copy-start | bytes 196612
  0.6 4.6 %copy-start.6 = (f32[4,128]{1,0:T(4,128)S(1)}, f32[4,128]{1,0:T(4,128)}, u32[]{:S(2)}) copy-start(f32[4,128]{1,0:T(4,128)} %rate_ref.2) | copy-start | bytes 6148
  0.7 4.6 %copy-start.1 = (f32[53,4,128]{2,1,0:T(4,128)S(1)}, f32[53,4,128]{2,1,0:T(4,128)}, u32[]{:S(2)}) copy-start(f32[53,4,128]{2,1,0:T(4,128)} %les_ref.1) | copy-start | bytes 325636
  0.7 4.6 %copy-start.4 = (f32[8192]{0:T(1024)S(1)}, f32[8192]{0:T(1024)}, u32[]{:S(2)}) copy-start(f32[8192]{0:T(1024)} %mass_ref.1) | copy-start | bytes 98308
  3.1 4.3 %collective-permute-start.1 = (f32[32,128]{1,0:T(8,128)S(1)}, f32[32,128]{1,0:T(8,128)S(1)}, u32[]{:S(2)}, u32[]{:S(2)}) collective-permute-start(f32[32,128]{1,0:T(8,128)S(1)} %get-tuple-element.11.edge_ref), channel_id=1, source_target_pairs={{0,8},{1,2},{2,1},{3,4},{4,3},{5,6},{6,5},{7,15},{8,0},{9,10},{10,... | collective-permute-start | bytes 49160 | tf_op jit(solution)/shard_map/ppermute | solution.py:334
  4.7 2.8 %collective-permute-start = (f32[32,128]{1,0:T(8,128)S(1)}, f32[32,128]{1,0:T(8,128)S(1)}, u32[]{:S(2)}, u32[]{:S(2)}) collective-permute-start(f32[32,128]{1,0:T(8,128)S(1)} %get-tuple-element.11.edge_ref), channel_id=1, source_target_pairs={{0,1},{1,0},{2,3},{3,2},{4,5},{5,4},{6,7},{7,6},{8,9},{9,8},{10,11... | collective-permute-start | bytes 49160 | tf_op jit(solution)/shard_map/ppermute | solution.py:334
  5.3 5.5 %copy-start.2 = (f32[3,53,53]{2,1,0:T(8,128)S(1)}, f32[3,53,53]{2,1,0:T(8,128)}, u32[]{:S(2)}) copy-start(f32[3,53,53]{2,1,0:T(8,128)} %rate_ref.3) | copy-start | bytes 101128
  5.3 5.5 %copy-start.3 = (f32[3,53,53]{2,1,0:T(8,128)S(1)}, f32[3,53,53]{2,1,0:T(8,128)}, u32[]{:S(2)}) copy-start(f32[3,53,53]{2,1,0:T(8,128)} %map_ref.1) | copy-start | bytes 101128
  5.3 5.5 %copy-start.5 = (s32[8192]{0:T(1024)S(1)}, s32[8192]{0:T(1024)}, u32[]{:S(2)}) copy-start(s32[8192]{0:T(1024)} %level_ref.1) | copy-start | bytes 98308
  7.8 7.4 %collective-permute-start.2 = (f32[120,256]{1,0:T(8,128)S(1)}, f32[120,256]{1,0:T(8,128)S(1)}, u32[]{:S(2)}, u32[]{:S(2)}) collective-permute-start(f32[120,256]{1,0:T(8,128)S(1)} %get-tuple-element.12.odd_ref), channel_id=1, source_target_pairs={{0,1},{1,0},{2,3},{3,2},{4,5},{5,4},{6,7},{7,6},{8,16},{9,17},{10,... | collective-permute-start | bytes 368648 | tf_op jit(solution)/shard_map/ppermute | solution.py:334
  10.7 5.0 %collective-permute-start.3 = (f32[120,256]{1,0:T(8,128)S(1)}, f32[120,256]{1,0:T(8,128)S(1)}, u32[]{:S(2)}, u32[]{:S(2)}) collective-permute-start(f32[120,256]{1,0:T(8,128)S(1)} %get-tuple-element.13.even_ref), channel_id=1, source_target_pairs={{0,8},{1,9},{2,10},{3,11},{4,12},{5,13},{6,14},{7,15},{8,0},{9,1},... | collective-permute-start | bytes 368648 | tf_op jit(solution)/shard_map/ppermute | solution.py:334

commit v5 on v4

--- a/solution.py
+++ b/solution.py
@@ -16,8 +16,10 @@
 BANDS = GROUPS + 1
 ROWBLOCK = 16
 EDGE = 64
+WIDTH = 4096
 CHUNK = 4096
 CHUNKS = (5120, 3072)
+STRETCHES = ((5120,), (1536, 1536))
 VMEM = pltpu.CompilerParams(vmem_limit_bytes=40 << 20)
 
 prior_weight = 16.0
@@ -96,9 +98,10 @@
     mass_ref, cell_ref, les_ref, rate_ref, cells_ref, w_ref, sems,
 ):
     pairs = [(les_hbm, les_ref), (rate_hbm, rate_ref), (cell_hbm, cell_ref), (mass_hbm, mass_ref)]
-    for start in range(0, NSP, ROWBLOCK):
-        at = pl.ds(start, min(ROWBLOCK, NSP - start))
-        pairs.append((comp_hbm.at[at], comp_ref.at[at]))
+    small = len(pairs)
+    for start in range(0, comp_ref.shape[1], WIDTH):
+        at = pl.ds(start, WIDTH)
+        pairs.append((comp_hbm.at[:, at], comp_ref.at[:, at]))
     copies = [pltpu.make_async_copy(src, dst, sems.at[i]) for i, (src, dst) in enumerate(pairs)]
     for copy in copies:
         copy.start()
@@ -110,11 +113,21 @@
     copies[1].wait()
     own_cells(les_ref, rate_ref, cells_ref)
     both = dot_nt(stacked(cells_ref[...]), place)
-    for copy in copies[2:]:
+    for copy in copies[2:small]:
         copy.wait()
-    w = weighted(comp_ref, mass_ref, w_ref)
-    band, index = band_and_index(*local_cells(cell_ref[...]))
-    both += dot_nt(w, hot(jnp.where(band == GROUPS, index, -1), EDGE))
+    w_ref[NSP + 1 :, :] = jnp.zeros((ROWS - NSP - 1, WIDTH), f32)
+
+    def body(i, total):
+        at = pl.ds(pl.multiple_of(i * WIDTH, WIDTH), WIDTH)
+        pltpu.make_async_copy(comp_hbm.at[:, at], comp_ref.at[:, at], sems.at[small + i]).wait()
+        mass = mass_ref[at].reshape(1, WIDTH)
+        w_ref[0:NSP, :] = comp_ref[:, at] * mass
+        w_ref[NSP : NSP + 1, :] = mass
+        band, index = band_and_index(*local_cells(cell_ref[:, at]))
+        place = hot(jnp.where(band == GROUPS, index, -1), EDGE)
+        return total + dot_nt(stacked(w_ref[...]), place)
+
+    both = lax.fori_loop(0, comp_ref.shape[1] // WIDTH, body, both)
     edge = both[0:ROWS] + both[ROWS:]
     if EDGE < 128:
         edge = jnp.concatenate([edge, jnp.zeros((ROWS, 128 - EDGE), f32)], axis=1)
@@ -279,10 +292,7 @@
     cells_ref[...] = full_ref[...].astype(bf16)
     mixed_ref[...] = jnp.zeros_like(mixed_ref)
     chunks = len(CHUNKS)
-
-    def copy_of(chunk):
-        at = pl.ds(sum(CHUNKS[:chunk]), CHUNKS[chunk])
-        return pltpu.make_async_copy(out_ref.at[:, at], updated_hbm.at[:, at], sems.at[1 + chunk])
+    sent = []
 
     for chunk in range(chunks):
         width = CHUNKS[chunk]
@@ -301,19 +311,30 @@
             [jnp.where(first, z[0:24], jnp.where(second, z[24:48], z[48:72])), z[72:104]], axis=0
         )
         source = jnp.concatenate([jnp.tanh(z), jnp.zeros((8, width), f32)], axis=0)
-        z = dot(maps_ref[...], three(source))
-        change = jnp.concatenate(
-            [
-                jnp.where(first, z[0:24], jnp.where(second, z[24:48], z[48:72])),
-                jnp.where(level == 2, z[72:104], 0.0),
-            ],
-            axis=0,
-        )
-        out_ref[:, at] = mixed_ref[0:NSP, 0:width] + change[0:NSP]
-        copy_of(chunk).start()
+        parts = three(source)
+        begin = 0
+        for stretch in STRETCHES[chunk]:
+            inside = slice(begin, begin + stretch)
+            z = dot(maps_ref[...], parts[:, inside])
+            one, two = first[:, inside], second[:, inside]
+            change = jnp.concatenate(
+                [
+                    jnp.where(one, z[0:24], jnp.where(two, z[24:48], z[48:72])),
+                    jnp.where(level[:, inside] == 2, z[72:104], 0.0),
+                ],
+                axis=0,
+            )
+            columns = pl.ds(sum(CHUNKS[:chunk]) + begin, stretch)
+            out_ref[:, columns] = mixed_ref[0:NSP, inside] + change[0:NSP]
+            out = pltpu.make_async_copy(
+                out_ref.at[:, columns], updated_hbm.at[:, columns], sems.at[1 + len(sent)]
+            )
+            out.start()
+            sent.append(out)
+            begin += stretch
     means_copy.wait()
-    for chunk in range(chunks):
-        copy_of(chunk).wait()
+    for out in sent:
+        out.wait()
 
 
 def swap(x, axis, odd):
@@ -361,8 +382,8 @@
             pltpu.VMEM(les_mean.shape, f32),
             pltpu.VMEM(mix_rate.shape, f32),
             prior,
-            pltpu.VMEM((ROWS, particles), f32),
-            pltpu.SemaphoreType.DMA((4 + pl.cdiv(NSP, ROWBLOCK),)),
+            pltpu.VMEM((ROWS, WIDTH), f32),
+            pltpu.SemaphoreType.DMA((4 + particles // WIDTH,)),
         ],
         compiler_params=VMEM,
         name="edge_sums",
@@ -410,7 +431,7 @@
             pltpu.VMEM(((BANDS + GROUPS) * ROWS, 2 * CY), bf16),
             pltpu.VMEM((64, max(CHUNKS)), f32),
             pltpu.VMEM(composition.shape, f32),
-            pltpu.SemaphoreType.DMA((len(CHUNKS) + 1,)),
+            pltpu.SemaphoreType.DMA((sum(map(len, STRETCHES)) + 1,)),
         ],
         compiler_params=VMEM,
         name="gather_react",

time: 20.6 us -> 20.4 us (level)
  transfers between devices with their start and end apart: 4 -> 4, of which waited for: 2 -> 2; matrix products, arithmetic and copies ran while one was open for 0% -> 0% of each run, Pallas kernels for 17% -> 18%
where the time goes in v5:
time: 20.4 us; the launch traced here: 20.3 us
  Pallas kernels  10.9 us (53%)
  starting transfers between devices  5.12 us (25%)
  waiting for transfers between devices  3.51 us (17%)
  between operations  0.73 us (4%)
    ppermute x4, starting transfers between devices, swap(): return lax.ppermute(x, ('gx', 'gy'), pairs)  5.12 us
    pallas_call x1, Pallas kernels, per_device(): pl.pallas_call(react_kernel, out_shape=(sds(composition.shape, f32), sds(...  4.71 us
    ppermute x4, waiting for transfers between devices, swap(): return lax.ppermute(x, ('gx', 'gy'), pairs)  3.51 us
    pallas_call x1, Pallas kernels, per_device(): pl.pallas_call(edge_kernel, out_shape=(sds((32, 128), f32), sds(compositi...  2.35 us
    pallas_call x1, Pallas kernels, per_device(): pl.pallas_call(main_kernel, out_shape=sds((GROUPS * ROWS, 2 * CY), f32),...  2.15 us
    pallas_call x1, Pallas kernels, per_device(): pl.pallas_call(prepare_kernel, out_shape=(sds((2 * CY, particles), bf16),...  1.41 us
  transfers between devices with their start and end apart: 4, of which 2 were waited for; matrix products, arithmetic and copies ran while one was open for 0% of the time, Pallas kernels for 18%

profile of v5, /device:TPU:24, one launch (start us, length us, event | category | flops | bytes accessed | tf_op | source)
XLA Modules:
  0.0 20.3 jit_solution(8798082041430933240)
XLA Ops:
  0.6 0.0 copy-start
  0.6 0.0 copy-start.6
  0.7 0.0 copy-start.1
  0.7 0.0 copy-start.4
  0.7 2.4 %edge_sums.1 = (f32[32,128]{1,0:T(8,128)S(1)}, f32[53,8192]{1,0:T(8,128)S(1)}) custom-call(f32[53,8192]{1,0:T(8,128)} %comp_hbm.1, f32[8192]{0:T(1024)} %mass_ref.1, s32[2,8192]{1,0:T(2,128)} %cell_ref.3, f32[53,4,128]{2,1,0:T(4,128)} %les_ref.1, f32[4,128]{1,0:T(4,128)} %rate_ref.2), custom_call_target="tpu_custom_call" | custom-call | tf_op jit(solution)/shard_map/edge_sums/pallas_call | solution.py:374
  3.0 1.6 %collective-permute-start.1 = (f32[32,128]{1,0:T(8,128)S(1)}, f32[32,128]{1,0:T(8,128)S(1)}, u32[]{:S(2)}, u32[]{:S(2)}) collective-permute-start(f32[32,128]{1,0:T(8,128)S(1)} %get-tuple-element.11.edge_ref), channel_id=1, source_target_pairs={{0,8},{1,2},{2,1},{3,4},{4,3},{5,6},{6,5},{7,15},{8,0},{9,10},{10,... | collective-permute-start | bytes 49160 | tf_op jit(solution)/shard_map/ppermute | solution.py:355
  4.6 0.5 %collective-permute-start = (f32[32,128]{1,0:T(8,128)S(1)}, f32[32,128]{1,0:T(8,128)S(1)}, u32[]{:S(2)}, u32[]{:S(2)}) collective-permute-start(f32[32,128]{1,0:T(8,128)S(1)} %get-tuple-element.11.edge_ref), channel_id=1, source_target_pairs={{0,1},{1,0},{2,3},{3,2},{4,5},{5,4},{6,7},{7,6},{8,9},{9,8},{10,11... | collective-permute-start | bytes 49160 | tf_op jit(solution)/shard_map/ppermute | solution.py:355
  5.1 0.0 copy-done
  5.1 0.0 copy-done.6
  5.2 0.0 copy-done.1
  5.2 0.0 copy-done.4
  5.2 0.0 copy-start.2
  5.2 0.0 copy-start.3
  5.2 0.0 copy-start.5
  5.2 2.2 %cell_sums.1.main_ref = f32[224,256]{1,0:T(8,128)S(1)} custom-call(f32[53,8192]{1,0:T(8,128)S(1)} %get-tuple-element.10.comp_ref, f32[8192]{0:T(1024)S(1)} %copy-done.4, s32[2,8192]{1,0:T(2,128)S(1)} %copy-done, f32[53,4,128]{2,1,0:T(4,128)S(1)} %copy-done.1, f32[4,128]{1,0:T(4,128)S(1)} %copy-done.6), custom_call_target="tpu_custom_call" | custom-call | flops 4294967296 | bytes 8388608 | tf_op jit(solution)/shard_map/cell_sums/pallas_call | solution.py:391
  7.4 0.0 collective-permute-done.1.odd_in_ref
  7.4 0.0 collective-permute-done.even_in_ref
  7.4 0.3 %pack.1 = (f32[120,256]{1,0:T(8,128)S(1)}, f32[120,256]{1,0:T(8,128)S(1)}) custom-call(f32[224,256]{1,0:T(8,128)S(1)} %cell_sums.1.main_ref, f32[32,128]{1,0:T(8,128)S(1)} %get-tuple-element.11.edge_ref, f32[32,128]{1,0:T(8,128)S(1)} %collective-permute-done.even_in_ref, f32[32,128]{1,0:T(8,128)S(1)} %collective-permute-done.1.odd_in_ref), custom_call_target="tpu_custom_call" | custom-call | tf_op jit(solution)/shard_map/pack/pallas_call | solution.py:404
  7.7 3.0 %collective-permute-start.2 = (f32[120,256]{1,0:T(8,128)S(1)}, f32[120,256]{1,0:T(8,128)S(1)}, u32[]{:S(2)}, u32[]{:S(2)}) collective-permute-start(f32[120,256]{1,0:T(8,128)S(1)} %get-tuple-element.12.odd_ref), channel_id=1, source_target_pairs={{0,1},{1,0},{2,3},{3,2},{4,5},{5,4},{6,7},{7,6},{8,16},{9,17},{10,... | collective-permute-start | bytes 368648 | tf_op jit(solution)/shard_map/ppermute | solution.py:355
  10.6 0.0 collective-permute-start.3
  10.7 0.0 copy-done.2
  10.7 0.0 copy-done.3
  10.7 0.0 copy-done.5
  10.7 1.4 %prepare.1 = (bf16[256,8192]{1,0:T(8,128)(2,1)S(1)}, s32[2,8192]{1,0:T(2,128)S(1)}, bf16[104,192]{1,0:T(8,128)(2,1)S(1)}, bf16[104,192]{1,0:T(8,128)(2,1)S(1)}) custom-call(s32[2,8192]{1,0:T(2,128)S(1)} %copy-done, s32[8192]{0:T(1024)S(1)} %copy-done.5, f32[3,53,53]{2,1,0:T(8,128)S(1)} %copy-done.2, f32[3,53,53]{2,1,0:T(8,128)S(1)} %copy-done.3), custom_call_target="tpu_custom_call" | custom-call | flops 4194304 | bytes 8388608 | tf_op jit(solution)/shard_map/prepare/pallas_call | solution.py:413
  12.1 3.0 %collective-permute-done.2.odd_in_ref = f32[120,256]{1,0:T(8,128)S(1)} collective-permute-done((f32[120,256]{1,0:T(8,128)S(1)}, f32[120,256]{1,0:T(8,128)S(1)}, u32[]{:S(2)}, u32[]{:S(2)}) %collective-permute-start.2) | collective-permute-done | bytes 122912 | tf_op jit(solution)/shard_map/ppermute | solution.py:355
  15.1 0.5 %collective-permute-done.3.even_in_ref = f32[120,256]{1,0:T(8,128)S(1)} collective-permute-done((f32[120,256]{1,0:T(8,128)S(1)}, f32[120,256]{1,0:T(8,128)S(1)}, u32[]{:S(2)}, u32[]{:S(2)}) %collective-permute-start.3) | collective-permute-done | bytes 122912 | tf_op jit(solution)/shard_map/ppermute | solution.py:355
  15.6 4.7 %gather_react.1 = (f32[53,8192]{1,0:T(8,128)}, f32[53,4,128]{2,1,0:T(4,128)}) custom-call(f32[120,256]{1,0:T(8,128)S(1)} %get-tuple-element.12.odd_ref, f32[120,256]{1,0:T(8,128)S(1)} %get-tuple-element.13.even_ref, f32[120,256]{1,0:T(8,128)S(1)} %collective-permute-done.2.odd_in_ref, f32[120,256]{1,0:T(8,128)S(1)} %collective-permute-done.3.even_in_ref, ...), custom_call_target="tpu_custom_call" | custom-call | tf_op jit(solution)/shard_map/gather_react/pallas_call | solution.py:423
Async XLA Ops:
  0.6 4.5 %copy-start = (s32[2,8192]{1,0:T(2,128)S(1)}, s32[2,8192]{1,0:T(2,128)}, u32[]{:S(2)}) copy-start(s32[2,8192]{1,0:T(2,128)} %cell_ref.3) | copy-start | bytes 196612
  0.6 4.5 %copy-start.6 = (f32[4,128]{1,0:T(4,128)S(1)}, f32[4,128]{1,0:T(4,128)}, u32[]{:S(2)}) copy-start(f32[4,128]{1,0:T(4,128)} %rate_ref.2) | copy-start | bytes 6148
  0.7 4.5 %copy-start.1 = (f32[53,4,128]{2,1,0:T(4,128)S(1)}, f32[53,4,128]{2,1,0:T(4,128)}, u32[]{:S(2)}) copy-start(f32[53,4,128]{2,1,0:T(4,128)} %les_ref.1) | copy-start | bytes 325636
  0.7 4.5 %copy-start.4 = (f32[8192]{0:T(1024)S(1)}, f32[8192]{0:T(1024)}, u32[]{:S(2)}) copy-start(f32[8192]{0:T(1024)} %mass_ref.1) | copy-start | bytes 98308
  3.0 4.3 %collective-permute-start.1 = (f32[32,128]{1,0:T(8,128)S(1)}, f32[32,128]{1,0:T(8,128)S(1)}, u32[]{:S(2)}, u32[]{:S(2)}) collective-permute-start(f32[32,128]{1,0:T(8,128)S(1)} %get-tuple-element.11.edge_ref), channel_id=1, source_target_pairs={{0,8},{1,2},{2,1},{3,4},{4,3},{5,6},{6,5},{7,15},{8,0},{9,10},{10,... | collective-permute-start | bytes 49160 | tf_op jit(solution)/shard_map/ppermute | solution.py:355
  4.6 2.8 %collective-permute-start = (f32[32,128]{1,0:T(8,128)S(1)}, f32[32,128]{1,0:T(8,128)S(1)}, u32[]{:S(2)}, u32[]{:S(2)}) collective-permute-start(f32[32,128]{1,0:T(8,128)S(1)} %get-tuple-element.11.edge_ref), channel_id=1, source_target_pairs={{0,1},{1,0},{2,3},{3,2},{4,5},{5,4},{6,7},{7,6},{8,9},{9,8},{10,11... | collective-permute-start | bytes 49160 | tf_op jit(solution)/shard_map/ppermute | solution.py:355
  5.2 5.5 %copy-start.2 = (f32[3,53,53]{2,1,0:T(8,128)S(1)}, f32[3,53,53]{2,1,0:T(8,128)}, u32[]{:S(2)}) copy-start(f32[3,53,53]{2,1,0:T(8,128)} %rate_ref.3) | copy-start | bytes 101128
  5.2 5.5 %copy-start.3 = (f32[3,53,53]{2,1,0:T(8,128)S(1)}, f32[3,53,53]{2,1,0:T(8,128)}, u32[]{:S(2)}) copy-start(f32[3,53,53]{2,1,0:T(8,128)} %map_ref.1) | copy-start | bytes 101128
  5.2 5.5 %copy-start.5 = (s32[8192]{0:T(1024)S(1)}, s32[8192]{0:T(1024)}, u32[]{:S(2)}) copy-start(s32[8192]{0:T(1024)} %level_ref.1) | copy-start | bytes 98308
  7.7 7.4 %collective-permute-start.2 = (f32[120,256]{1,0:T(8,128)S(1)}, f32[120,256]{1,0:T(8,128)S(1)}, u32[]{:S(2)}, u32[]{:S(2)}) collective-permute-start(f32[120,256]{1,0:T(8,128)S(1)} %get-tuple-element.12.odd_ref), channel_id=1, source_target_pairs={{0,1},{1,0},{2,3},{3,2},{4,5},{5,4},{6,7},{7,6},{8,16},{9,17},{10,... | collective-permute-start | bytes 368648 | tf_op jit(solution)/shard_map/ppermute | solution.py:355
  10.6 5.0 %collective-permute-start.3 = (f32[120,256]{1,0:T(8,128)S(1)}, f32[120,256]{1,0:T(8,128)S(1)}, u32[]{:S(2)}, u32[]{:S(2)}) collective-permute-start(f32[120,256]{1,0:T(8,128)S(1)} %get-tuple-element.13.even_ref), channel_id=1, source_target_pairs={{0,8},{1,9},{2,10},{3,11},{4,12},{5,13},{6,14},{7,15},{8,0},{9,1},... | collective-permute-start | bytes 368648 | tf_op jit(solution)/shard_map/ppermute | solution.py:355

commit v6 on v5

--- a/solution.py
+++ b/solution.py
@@ -371,16 +371,19 @@
     hbm = pl.BlockSpec(memory_space=pltpu.HBM)
     vmem = pl.BlockSpec(memory_space=pltpu.VMEM)
     prior = pltpu.VMEM((ROWS, CX * CY), f32)
-    edge, local = pl.pallas_call(
+    edge, local, mass, cell, les, rate = pl.pallas_call(
         edge_kernel,
-        out_shape=(sds((32, 128), f32), sds(composition.shape, f32)),
+        out_shape=(
+            sds((32, 128), f32),
+            sds(composition.shape, f32),
+            sds(particle_mass.shape, f32),
+            sds(particle_cell.shape, jnp.int32),
+            sds(les_mean.shape, f32),
+            sds(mix_rate.shape, f32),
+        ),
         in_specs=[hbm] * 5,
-        out_specs=(vmem, vmem),
+        out_specs=(vmem,) * 6,
         scratch_shapes=[
-            pltpu.VMEM(particle_mass.shape, f32),
-            pltpu.VMEM(particle_cell.shape, jnp.int32),
-            pltpu.VMEM(les_mean.shape, f32),
-            pltpu.VMEM(mix_rate.shape, f32),
             prior,
             pltpu.VMEM((ROWS, WIDTH), f32),
             pltpu.SemaphoreType.DMA((4 + particles // WIDTH,)),
@@ -397,7 +400,7 @@
         compiler_params=VMEM,
         cost_estimate=pl.CostEstimate(flops=1 << 32, bytes_accessed=8 << 20, transcendentals=0),
         name="cell_sums",
-    )(local, particle_mass, particle_cell, les_mean, mix_rate)
+    )(local, mass, cell, les, rate)
     edge_even = swap(edge, "gy", 0)
     edge_odd = swap(edge, "gy", 1)
     payload = sds((2 * ROWS + 8, 2 * CY), f32)
@@ -419,7 +422,7 @@
         compiler_params=VMEM,
         cost_estimate=pl.CostEstimate(flops=1 << 22, bytes_accessed=8 << 20, transcendentals=0),
         name="prepare",
-    )(particle_cell, particle_level, rate_matrix, implicit_map)
+    )(cell, particle_level, rate_matrix, implicit_map)
     return pl.pallas_call(
         react_kernel,
         out_shape=(sds(composition.shape, f32), sds(les_mean.shape, f32)),

time: 20.4 us -> 20.3 us (level)
  no operation moved by 1% of the time
where the time goes in v6:
time: 20.3 us; the launch traced here: 20.2 us
  Pallas kernels  10.9 us (54%)
  starting transfers between devices  5.13 us (25%)
  waiting for transfers between devices  3.5 us (17%)
  between operations  0.68 us (3%)
    ppermute x4, starting transfers between devices, swap(): return lax.ppermute(x, ('gx', 'gy'), pairs)  5.13 us
    pallas_call x1, Pallas kernels, per_device(): pl.pallas_call(react_kernel, out_shape=(sds(composition.shape, f32), sds(...  4.7 us
    ppermute x4, waiting for transfers between devices, swap(): return lax.ppermute(x, ('gx', 'gy'), pairs)  3.5 us
    pallas_call x1, Pallas kernels, per_device(): pl.pallas_call(edge_kernel, out_shape=(sds((32, 128), f32), sds(compositi...  2.33 us
    pallas_call x1, Pallas kernels, per_device(): pl.pallas_call(main_kernel, out_shape=sds((GROUPS * ROWS, 2 * CY), f32),...  2.15 us
    pallas_call x1, Pallas kernels, per_device(): pl.pallas_call(prepare_kernel, out_shape=(sds((2 * CY, particles), bf16),...  1.41 us
  transfers between devices with their start and end apart: 4, of which 2 were waited for; matrix products, arithmetic and copies ran while one was open for 0% of the time, Pallas kernels for 18%

profile of v6, /device:TPU:24, one launch (start us, length us, event | category | flops | bytes accessed | tf_op | source)
XLA Modules:
  0.0 20.2 jit_solution(16561445962623229902)
XLA Ops:
  0.6 2.3 %edge_sums.1 = (f32[32,128]{1,0:T(8,128)S(1)}, f32[53,8192]{1,0:T(8,128)S(1)}, f32[8192]{0:T(1024)S(1)}, s32[2,8192]{1,0:T(2,128)S(1)}, f32[53,4,128]{2,1,0:T(4,128)S(1)}, /*index=5*/f32[4,128]{1,0:T(4,128)S(1)}) custom-call(f32[53,8192]{1,0:T(8,128)} %comp_hbm.1, f32[8192]{0:T(1024)} %mass_hbm.1, s32[2,8192]{1,0:T(2,128)} %cell_hbm.1, ...), custom_call_target="tpu_custom_call" | custom-call | tf_op jit(solution)/shard_map/edge_sums/pallas_call | solution.py:374
  3.0 1.6 %collective-permute-start.1 = (f32[32,128]{1,0:T(8,128)S(1)}, f32[32,128]{1,0:T(8,128)S(1)}, u32[]{:S(2)}, u32[]{:S(2)}) collective-permute-start(f32[32,128]{1,0:T(8,128)S(1)} %get-tuple-element.19.edge_ref), channel_id=1, source_target_pairs={{0,8},{1,2},{2,1},{3,4},{4,3},{5,6},{6,5},{7,15},{8,0},{9,10},{10,... | collective-permute-start | bytes 49160 | tf_op jit(solution)/shard_map/ppermute | solution.py:355
  4.5 0.5 %collective-permute-start = (f32[32,128]{1,0:T(8,128)S(1)}, f32[32,128]{1,0:T(8,128)S(1)}, u32[]{:S(2)}, u32[]{:S(2)}) collective-permute-start(f32[32,128]{1,0:T(8,128)S(1)} %get-tuple-element.19.edge_ref), channel_id=1, source_target_pairs={{0,1},{1,0},{2,3},{3,2},{4,5},{5,4},{6,7},{7,6},{8,9},{9,8},{10,11... | collective-permute-start | bytes 49160 | tf_op jit(solution)/shard_map/ppermute | solution.py:355
  5.1 0.0 copy-start
  5.1 0.0 copy-start.1
  5.1 0.0 copy-start.2
  5.1 2.1 %cell_sums.1.main_ref = f32[224,256]{1,0:T(8,128)S(1)} custom-call(f32[53,8192]{1,0:T(8,128)S(1)} %get-tuple-element.14.comp_ref, f32[8192]{0:T(1024)S(1)} %get-tuple-element.15.mass_ref, s32[2,8192]{1,0:T(2,128)S(1)} %get-tuple-element.16.cell_ref, f32[53,4,128]{2,1,0:T(4,128)S(1)} %get-tuple-element.17.les_ref, f32[4,128]{1,0:T(4,128)S(1)} %get-tuple-element.18.rate_ref), custom_call_target="tpu_custom_call" | custom-call | flops 4294967296 | bytes 8388608 | tf_op jit(solution)/shard_map/cell_sums/pallas_call | solution.py:394
  7.2 0.0 collective-permute-done.1.odd_in_ref
  7.3 0.0 collective-permute-done.even_in_ref
  7.3 0.3 %pack.1 = (f32[120,256]{1,0:T(8,128)S(1)}, f32[120,256]{1,0:T(8,128)S(1)}) custom-call(f32[224,256]{1,0:T(8,128)S(1)} %cell_sums.1.main_ref, f32[32,128]{1,0:T(8,128)S(1)} %get-tuple-element.19.edge_ref, f32[32,128]{1,0:T(8,128)S(1)} %collective-permute-done.even_in_ref, f32[32,128]{1,0:T(8,128)S(1)} %collective-permute-done.1.odd_in_ref), custom_call_target="tpu_custom_call" | custom-call | tf_op jit(solution)/shard_map/pack/pallas_call | solution.py:407
  7.6 3.0 %collective-permute-start.2 = (f32[120,256]{1,0:T(8,128)S(1)}, f32[120,256]{1,0:T(8,128)S(1)}, u32[]{:S(2)}, u32[]{:S(2)}) collective-permute-start(f32[120,256]{1,0:T(8,128)S(1)} %get-tuple-element.20.odd_ref), channel_id=1, source_target_pairs={{0,1},{1,0},{2,3},{3,2},{4,5},{5,4},{6,7},{7,6},{8,16},{9,17},{10,... | collective-permute-start | bytes 368648 | tf_op jit(solution)/shard_map/ppermute | solution.py:355
  10.5 0.0 collective-permute-start.3
  10.6 0.0 copy-done
  10.6 0.0 copy-done.1
  10.6 0.0 copy-done.2
  10.6 1.4 %prepare.1 = (bf16[256,8192]{1,0:T(8,128)(2,1)S(1)}, s32[2,8192]{1,0:T(2,128)S(1)}, bf16[104,192]{1,0:T(8,128)(2,1)S(1)}, bf16[104,192]{1,0:T(8,128)(2,1)S(1)}) custom-call(s32[2,8192]{1,0:T(2,128)S(1)} %get-tuple-element.16.cell_ref, s32[8192]{0:T(1024)S(1)} %copy-done.2, f32[3,53,53]{2,1,0:T(8,128)S(1)} %copy-done, f32[3,53,53]{2,1,0:T(8,128)S(1)} %copy-done.1), custom_call_target="tpu_custom_call" | custom-call | flops 4194304 | bytes 8388608 | tf_op jit(solution)/shard_map/prepare/pallas_call | solution.py:416
  12.0 2.9 %collective-permute-done.2.odd_in_ref = f32[120,256]{1,0:T(8,128)S(1)} collective-permute-done((f32[120,256]{1,0:T(8,128)S(1)}, f32[120,256]{1,0:T(8,128)S(1)}, u32[]{:S(2)}, u32[]{:S(2)}) %collective-permute-start.2) | collective-permute-done | bytes 122912 | tf_op jit(solution)/shard_map/ppermute | solution.py:355
  14.9 0.6 %collective-permute-done.3.even_in_ref = f32[120,256]{1,0:T(8,128)S(1)} collective-permute-done((f32[120,256]{1,0:T(8,128)S(1)}, f32[120,256]{1,0:T(8,128)S(1)}, u32[]{:S(2)}, u32[]{:S(2)}) %collective-permute-start.3) | collective-permute-done | bytes 122912 | tf_op jit(solution)/shard_map/ppermute | solution.py:355
  15.5 4.7 %gather_react.1 = (f32[53,8192]{1,0:T(8,128)}, f32[53,4,128]{2,1,0:T(4,128)}) custom-call(f32[120,256]{1,0:T(8,128)S(1)} %get-tuple-element.20.odd_ref, f32[120,256]{1,0:T(8,128)S(1)} %get-tuple-element.21.even_ref, f32[120,256]{1,0:T(8,128)S(1)} %collective-permute-done.2.odd_in_ref, f32[120,256]{1,0:T(8,128)S(1)} %collective-permute-done.3.even_in_ref, ...), custom_call_target="tpu_custom_call" | custom-call | tf_op jit(solution)/shard_map/gather_react/pallas_call | solution.py:426
Async XLA Ops:
  3.0 4.3 %collective-permute-start.1 = (f32[32,128]{1,0:T(8,128)S(1)}, f32[32,128]{1,0:T(8,128)S(1)}, u32[]{:S(2)}, u32[]{:S(2)}) collective-permute-start(f32[32,128]{1,0:T(8,128)S(1)} %get-tuple-element.19.edge_ref), channel_id=1, source_target_pairs={{0,8},{1,2},{2,1},{3,4},{4,3},{5,6},{6,5},{7,15},{8,0},{9,10},{10,... | collective-permute-start | bytes 49160 | tf_op jit(solution)/shard_map/ppermute | solution.py:355
  4.5 2.7 %collective-permute-start = (f32[32,128]{1,0:T(8,128)S(1)}, f32[32,128]{1,0:T(8,128)S(1)}, u32[]{:S(2)}, u32[]{:S(2)}) collective-permute-start(f32[32,128]{1,0:T(8,128)S(1)} %get-tuple-element.19.edge_ref), channel_id=1, source_target_pairs={{0,1},{1,0},{2,3},{3,2},{4,5},{5,4},{6,7},{7,6},{8,9},{9,8},{10,11... | collective-permute-start | bytes 49160 | tf_op jit(solution)/shard_map/ppermute | solution.py:355
  5.1 5.5 %copy-start = (f32[3,53,53]{2,1,0:T(8,128)S(1)}, f32[3,53,53]{2,1,0:T(8,128)}, u32[]{:S(2)}) copy-start(f32[3,53,53]{2,1,0:T(8,128)} %rate_ref.1) | copy-start | bytes 101128
  5.1 5.5 %copy-start.1 = (f32[3,53,53]{2,1,0:T(8,128)S(1)}, f32[3,53,53]{2,1,0:T(8,128)}, u32[]{:S(2)}) copy-start(f32[3,53,53]{2,1,0:T(8,128)} %map_ref.1) | copy-start | bytes 101128
  5.1 5.5 %copy-start.2 = (s32[8192]{0:T(1024)S(1)}, s32[8192]{0:T(1024)}, u32[]{:S(2)}) copy-start(s32[8192]{0:T(1024)} %level_ref.1) | copy-start | bytes 98308
  7.6 7.4 %collective-permute-start.2 = (f32[120,256]{1,0:T(8,128)S(1)}, f32[120,256]{1,0:T(8,128)S(1)}, u32[]{:S(2)}, u32[]{:S(2)}) collective-permute-start(f32[120,256]{1,0:T(8,128)S(1)} %get-tuple-element.20.odd_ref), channel_id=1, source_target_pairs={{0,1},{1,0},{2,3},{3,2},{4,5},{5,4},{6,7},{7,6},{8,16},{9,17},{10,... | collective-permute-start | bytes 368648 | tf_op jit(solution)/shard_map/ppermute | solution.py:355
  10.5 5.0 %collective-permute-start.3 = (f32[120,256]{1,0:T(8,128)S(1)}, f32[120,256]{1,0:T(8,128)S(1)}, u32[]{:S(2)}, u32[]{:S(2)}) collective-permute-start(f32[120,256]{1,0:T(8,128)S(1)} %get-tuple-element.21.even_ref), channel_id=1, source_target_pairs={{0,8},{1,9},{2,10},{3,11},{4,12},{5,13},{6,14},{7,15},{8,0},{9,1},... | collective-permute-start | bytes 368648 | tf_op jit(solution)/shard_map/ppermute | solution.py:355

commit v7 on v6

--- a/solution.py
+++ b/solution.py
@@ -103,8 +103,8 @@
         at = pl.ds(start, WIDTH)
         pairs.append((comp_hbm.at[:, at], comp_ref.at[:, at]))
     copies = [pltpu.make_async_copy(src, dst, sems.at[i]) for i, (src, dst) in enumerate(pairs)]
-    for copy in copies:
-        copy.start()
+    for i in (0, 1, 4, 2, 3, *range(5, len(copies))):
+        copies[i].start()
     cells = CX * CY
     cell = lax.broadcasted_iota(jnp.int32, (1, cells), 1)
     band, index = band_and_index(cell // CY + R, cell % CY + R)

time: 20.3 us -> 20.3 us (level)
  no operation moved by 1% of the time
where the time goes in v7:
time: 20.3 us; the launch traced here: 20.1 us
  Pallas kernels  10.8 us (53%)
  starting transfers between devices  5.13 us (25%)
  waiting for transfers between devices  3.5 us (17%)
  between operations  0.68 us (3%)
    ppermute x4, starting transfers between devices, swap(): return lax.ppermute(x, ('gx', 'gy'), pairs)  5.13 us
    pallas_call x1, Pallas kernels, per_device(): pl.pallas_call(react_kernel, out_shape=(sds(composition.shape, f32), sds(...  4.69 us
    ppermute x4, waiting for transfers between devices, swap(): return lax.ppermute(x, ('gx', 'gy'), pairs)  3.5 us
    pallas_call x1, Pallas kernels, per_device(): pl.pallas_call(edge_kernel, out_shape=(sds((32, 128), f32), sds(compositi...  2.27 us
    pallas_call x1, Pallas kernels, per_device(): pl.pallas_call(main_kernel, out_shape=sds((GROUPS * ROWS, 2 * CY), f32),...  2.15 us
    pallas_call x1, Pallas kernels, per_device(): pl.pallas_call(prepare_kernel, out_shape=(sds((2 * CY, particles), bf16),...  1.41 us
  transfers between devices with their start and end apart: 4, of which 2 were waited for; matrix products, arithmetic and copies ran while one was open for 0% of the time, Pallas kernels for 18%

profile of v7, /device:TPU:24, one launch (start us, length us, event | category | flops | bytes accessed | tf_op | source)
XLA Modules:
  0.0 20.1 jit_solution(13008776352461419890)
XLA Ops:
  0.6 2.3 %edge_sums.1 = (f32[32,128]{1,0:T(8,128)S(1)}, f32[53,8192]{1,0:T(8,128)S(1)}, f32[8192]{0:T(1024)S(1)}, s32[2,8192]{1,0:T(2,128)S(1)}, f32[53,4,128]{2,1,0:T(4,128)S(1)}, /*index=5*/f32[4,128]{1,0:T(4,128)S(1)}) custom-call(f32[53,8192]{1,0:T(8,128)} %comp_hbm.1, f32[8192]{0:T(1024)} %mass_hbm.1, s32[2,8192]{1,0:T(2,128)} %cell_hbm.1, ...), custom_call_target="tpu_custom_call" | custom-call | tf_op jit(solution)/shard_map/edge_sums/pallas_call | solution.py:374
  2.9 1.6 %collective-permute-start.1 = (f32[32,128]{1,0:T(8,128)S(1)}, f32[32,128]{1,0:T(8,128)S(1)}, u32[]{:S(2)}, u32[]{:S(2)}) collective-permute-start(f32[32,128]{1,0:T(8,128)S(1)} %get-tuple-element.19.edge_ref), channel_id=1, source_target_pairs={{0,8},{1,2},{2,1},{3,4},{4,3},{5,6},{6,5},{7,15},{8,0},{9,10},{10,... | collective-permute-start | bytes 49160 | tf_op jit(solution)/shard_map/ppermute | solution.py:355
  4.5 0.5 %collective-permute-start = (f32[32,128]{1,0:T(8,128)S(1)}, f32[32,128]{1,0:T(8,128)S(1)}, u32[]{:S(2)}, u32[]{:S(2)}) collective-permute-start(f32[32,128]{1,0:T(8,128)S(1)} %get-tuple-element.19.edge_ref), channel_id=1, source_target_pairs={{0,1},{1,0},{2,3},{3,2},{4,5},{5,4},{6,7},{7,6},{8,9},{9,8},{10,11... | collective-permute-start | bytes 49160 | tf_op jit(solution)/shard_map/ppermute | solution.py:355
  5.0 0.0 copy-start
  5.0 0.0 copy-start.1
  5.0 0.0 copy-start.2
  5.0 2.1 %cell_sums.1.main_ref = f32[224,256]{1,0:T(8,128)S(1)} custom-call(f32[53,8192]{1,0:T(8,128)S(1)} %get-tuple-element.14.comp_ref, f32[8192]{0:T(1024)S(1)} %get-tuple-element.15.mass_ref, s32[2,8192]{1,0:T(2,128)S(1)} %get-tuple-element.16.cell_ref, f32[53,4,128]{2,1,0:T(4,128)S(1)} %get-tuple-element.17.les_ref, f32[4,128]{1,0:T(4,128)S(1)} %get-tuple-element.18.rate_ref), custom_call_target="tpu_custom_call" | custom-call | flops 4294967296 | bytes 8388608 | tf_op jit(solution)/shard_map/cell_sums/pallas_call | solution.py:394
  7.2 0.0 collective-permute-done.1.odd_in_ref
  7.2 0.0 collective-permute-done.even_in_ref
  7.2 0.3 %pack.1 = (f32[120,256]{1,0:T(8,128)S(1)}, f32[120,256]{1,0:T(8,128)S(1)}) custom-call(f32[224,256]{1,0:T(8,128)S(1)} %cell_sums.1.main_ref, f32[32,128]{1,0:T(8,128)S(1)} %get-tuple-element.19.edge_ref, f32[32,128]{1,0:T(8,128)S(1)} %collective-permute-done.even_in_ref, f32[32,128]{1,0:T(8,128)S(1)} %collective-permute-done.1.odd_in_ref), custom_call_target="tpu_custom_call" | custom-call | tf_op jit(solution)/shard_map/pack/pallas_call | solution.py:407
  7.5 3.0 %collective-permute-start.2 = (f32[120,256]{1,0:T(8,128)S(1)}, f32[120,256]{1,0:T(8,128)S(1)}, u32[]{:S(2)}, u32[]{:S(2)}) collective-permute-start(f32[120,256]{1,0:T(8,128)S(1)} %get-tuple-element.20.odd_ref), channel_id=1, source_target_pairs={{0,1},{1,0},{2,3},{3,2},{4,5},{5,4},{6,7},{7,6},{8,16},{9,17},{10,... | collective-permute-start | bytes 368648 | tf_op jit(solution)/shard_map/ppermute | solution.py:355
  10.5 0.0 collective-permute-start.3
  10.5 0.0 copy-done
  10.5 0.0 copy-done.1
  10.5 0.0 copy-done.2
  10.5 1.4 %prepare.1 = (bf16[256,8192]{1,0:T(8,128)(2,1)S(1)}, s32[2,8192]{1,0:T(2,128)S(1)}, bf16[104,192]{1,0:T(8,128)(2,1)S(1)}, bf16[104,192]{1,0:T(8,128)(2,1)S(1)}) custom-call(s32[2,8192]{1,0:T(2,128)S(1)} %get-tuple-element.16.cell_ref, s32[8192]{0:T(1024)S(1)} %copy-done.2, f32[3,53,53]{2,1,0:T(8,128)S(1)} %copy-done, f32[3,53,53]{2,1,0:T(8,128)S(1)} %copy-done.1), custom_call_target="tpu_custom_call" | custom-call | flops 4194304 | bytes 8388608 | tf_op jit(solution)/shard_map/prepare/pallas_call | solution.py:416
  11.9 2.9 %collective-permute-done.2.odd_in_ref = f32[120,256]{1,0:T(8,128)S(1)} collective-permute-done((f32[120,256]{1,0:T(8,128)S(1)}, f32[120,256]{1,0:T(8,128)S(1)}, u32[]{:S(2)}, u32[]{:S(2)}) %collective-permute-start.2) | collective-permute-done | bytes 122912 | tf_op jit(solution)/shard_map/ppermute | solution.py:355
  14.9 0.6 %collective-permute-done.3.even_in_ref = f32[120,256]{1,0:T(8,128)S(1)} collective-permute-done((f32[120,256]{1,0:T(8,128)S(1)}, f32[120,256]{1,0:T(8,128)S(1)}, u32[]{:S(2)}, u32[]{:S(2)}) %collective-permute-start.3) | collective-permute-done | bytes 122912 | tf_op jit(solution)/shard_map/ppermute | solution.py:355
  15.4 4.7 %gather_react.1 = (f32[53,8192]{1,0:T(8,128)}, f32[53,4,128]{2,1,0:T(4,128)}) custom-call(f32[120,256]{1,0:T(8,128)S(1)} %get-tuple-element.20.odd_ref, f32[120,256]{1,0:T(8,128)S(1)} %get-tuple-element.21.even_ref, f32[120,256]{1,0:T(8,128)S(1)} %collective-permute-done.2.odd_in_ref, f32[120,256]{1,0:T(8,128)S(1)} %collective-permute-done.3.even_in_ref, ...), custom_call_target="tpu_custom_call" | custom-call | tf_op jit(solution)/shard_map/gather_react/pallas_call | solution.py:426
Async XLA Ops:
  2.9 4.3 %collective-permute-start.1 = (f32[32,128]{1,0:T(8,128)S(1)}, f32[32,128]{1,0:T(8,128)S(1)}, u32[]{:S(2)}, u32[]{:S(2)}) collective-permute-start(f32[32,128]{1,0:T(8,128)S(1)} %get-tuple-element.19.edge_ref), channel_id=1, source_target_pairs={{0,8},{1,2},{2,1},{3,4},{4,3},{5,6},{6,5},{7,15},{8,0},{9,10},{10,... | collective-permute-start | bytes 49160 | tf_op jit(solution)/shard_map/ppermute | solution.py:355
  4.5 2.7 %collective-permute-start = (f32[32,128]{1,0:T(8,128)S(1)}, f32[32,128]{1,0:T(8,128)S(1)}, u32[]{:S(2)}, u32[]{:S(2)}) collective-permute-start(f32[32,128]{1,0:T(8,128)S(1)} %get-tuple-element.19.edge_ref), channel_id=1, source_target_pairs={{0,1},{1,0},{2,3},{3,2},{4,5},{5,4},{6,7},{7,6},{8,9},{9,8},{10,11... | collective-permute-start | bytes 49160 | tf_op jit(solution)/shard_map/ppermute | solution.py:355
  5.0 5.5 %copy-start = (f32[3,53,53]{2,1,0:T(8,128)S(1)}, f32[3,53,53]{2,1,0:T(8,128)}, u32[]{:S(2)}) copy-start(f32[3,53,53]{2,1,0:T(8,128)} %rate_ref.1) | copy-start | bytes 101128
  5.0 5.5 %copy-start.1 = (f32[3,53,53]{2,1,0:T(8,128)S(1)}, f32[3,53,53]{2,1,0:T(8,128)}, u32[]{:S(2)}) copy-start(f32[3,53,53]{2,1,0:T(8,128)} %map_ref.1) | copy-start | bytes 101128
  5.0 5.5 %copy-start.2 = (s32[8192]{0:T(1024)S(1)}, s32[8192]{0:T(1024)}, u32[]{:S(2)}) copy-start(s32[8192]{0:T(1024)} %level_ref.1) | copy-start | bytes 98308
  7.5 7.4 %collective-permute-start.2 = (f32[120,256]{1,0:T(8,128)S(1)}, f32[120,256]{1,0:T(8,128)S(1)}, u32[]{:S(2)}, u32[]{:S(2)}) collective-permute-start(f32[120,256]{1,0:T(8,128)S(1)} %get-tuple-element.20.odd_ref), channel_id=1, source_target_pairs={{0,1},{1,0},{2,3},{3,2},{4,5},{5,4},{6,7},{7,6},{8,16},{9,17},{10,... | collective-permute-start | bytes 368648 | tf_op jit(solution)/shard_map/ppermute | solution.py:355
  10.5 5.0 %collective-permute-start.3 = (f32[120,256]{1,0:T(8,128)S(1)}, f32[120,256]{1,0:T(8,128)S(1)}, u32[]{:S(2)}, u32[]{:S(2)}) collective-permute-start(f32[120,256]{1,0:T(8,128)S(1)} %get-tuple-element.21.even_ref), channel_id=1, source_target_pairs={{0,8},{1,9},{2,10},{3,11},{4,12},{5,13},{6,14},{7,15},{8,0},{9,1},... | collective-permute-start | bytes 368648 | tf_op jit(solution)/shard_map/ppermute | solution.py:355
